TPU v7x, 512 devices: a whole 4x8x8 slice. The times are simulated.
512 devices in a mesh: branch: 64 (over z, y), sub: 8 (over x, core).
Axes of the slice: x: 4, y: 8, z: 8, core: 2. Of those that a mesh axis runs over, the one named last changes fastest.
Arguments:
- vectors: float32 [64, 2097152], P(None, ('branch', 'sub')), may hold values from -1.6 to 1.6
- coords: float32 [2, 2097152], P(None, ('branch', 'sub')), may hold values from 0 to 3
- basis: float32 [32, 2097152], P(None, ('branch', 'sub')), may hold values from -0.5 to 0.5
- leaf_transfer: float32 [16384, 32, 32], P(('branch', 'sub')), may hold values from -1 to 1
- node_transfer: float32 [512, 32, 32], P(('branch', 'sub')), may hold values from -0.375 to 0.375
- skel_one: float32 [512, 2, 32], P(('branch', 'sub')), may hold values from 0 to 3
- skel_two: float32 [64, 2, 32], replicated, may hold values from 0 to 3
- near_list: int32 [16384, 9], P(('branch', 'sub')), may hold values from 0 to 16383, as said below
- list_one: int32 [512, 8], P(('branch', 'sub')), may hold values from 0 to 511, as said below
- list_two: int32 [64, 8], P('branch'), may hold values from 0 to 63
Outputs:
- product: float32 [64, 2097152], P(None, ('branch', 'sub'))
Inputs may be any that keep to these rules, and one draw needn't show every extreme that they name: `near_list`: entry 0 of each row is the leaf itself. Every entry names a leaf of the same sub-branch, or of the sub-branch one branch index lower or higher with the same sub index (the leaf numbered (b * 8 + s) * 32 + i lies in branch group b, sub-branch s); those of the lower one are among its last 8 leaves, those of the higher one among its first 8, and in every draw some leaf names the first of those last 8 and some the last of those first 8. `list_one`: node n = b * 8 + s names only nodes with the same sub index s.
All inputs are finite; a program needn't handle non-finite values.
Results may differ from a plain program's by a relative error of at most 0.00015.
Values sent between devices are 32-bit elements; how exact they have to be, the bound alone decides.
A program may use at most 64 MiB of HBM per device.

v0:
```python
import jax
import jax.numpy as jnp
from jax import lax
from jax.sharding import PartitionSpec as P

NUGGET = 0.5
LENGTH_SCALE = 0.7
ROOT_THREE = 1.7320508075688772


def with_halo(cells, sides, width):
    for axis, dim in sides:
        count = lax.axis_size(axis)
        ends = count - 1
        head = lax.slice_in_dim(cells, 0, width, axis=dim)
        tail = lax.slice_in_dim(cells, cells.shape[dim] - width, cells.shape[dim], axis=dim)
        cells = jnp.concatenate(
            [
                lax.ppermute(tail, axis, [(i, (i + 1) % count) for i in range(ends)]),
                cells,
                lax.ppermute(head, axis, [((i + 1) % count, i) for i in range(ends)]),
            ],
            axis=dim,
        )
    return cells


def matern(target, source):
    delta_x = target[..., 0, :, None] - source[..., 0, None, :]
    delta_y = target[..., 1, :, None] - source[..., 1, None, :]
    distance = jnp.sqrt(delta_x * delta_x + delta_y * delta_y)
    scaled = ROOT_THREE / LENGTH_SCALE * distance
    return (1.0 + scaled) * jnp.exp(-scaled)


def far_terms(target, sources, coeffs, listed):
    precise = lax.Precision.HIGHEST
    row_count = coeffs.shape[0]
    one_hot = (listed[:, None] == jnp.arange(row_count, dtype=jnp.int32)[None, :]).astype(
        jnp.float32
    )
    picked_points = jnp.einsum("kr,rdj->kdj", one_hot, sources, precision=precise)
    picked_coeffs = jnp.einsum("kr,rjv->kjv", one_hot, coeffs, precision=precise)
    kernel_tile = matern(target, picked_points)
    return jnp.einsum("kij,kjv->iv", kernel_tile, picked_coeffs, precision=precise)


def body(
    vectors,
    coords,
    basis,
    leaf_transfer,
    node_transfer,
    skel_one,
    skel_two,
    near_list,
    list_one,
    list_two,
):
    precise = lax.Precision.HIGHEST
    vec_count, columns = vectors.shape
    rank_size = basis.shape[0]
    leaves = leaf_transfer.shape[0]
    leaf_size = columns // leaves
    sub_count = lax.axis_size("sub")
    group_index = lax.axis_index("branch")
    leaf_vecs = vectors.reshape(vec_count, leaves, leaf_size)
    leaf_basis = basis.reshape(rank_size, leaves, leaf_size)
    coeff_leaf = jnp.einsum("rlp,vlp->lrv", leaf_basis, leaf_vecs, precision=precise)
    coeff_node = jnp.einsum("lqr,lqv->rv", leaf_transfer, coeff_leaf, precision=precise)
    upward = jnp.einsum("qr,qv->rv", node_transfer[0], coeff_node, precision=precise)
    source_branch = list_one[0] // sub_count
    group_target = lax.dynamic_index_in_dim(skel_two, group_index, 0, keepdims=False)
    node_far = far_terms(
        skel_one[0],
        lax.all_gather(skel_one, "branch", axis=0, tiled=True),
        lax.all_gather(coeff_node[None], "branch", axis=0, tiled=True),
        source_branch,
    )
    coeff_group = lax.psum(upward, "sub")
    field_group = far_terms(
        group_target,
        skel_two,
        lax.all_gather(coeff_group[None], "branch", axis=0, tiled=True),
        list_two[0],
    )
    field_node = node_far + jnp.einsum(
        "rq,qv->rv", node_transfer[0], field_group, precision=precise
    )
    field_leaf = jnp.einsum("lrq,qv->lrv", leaf_transfer, field_node, precision=precise)
    far_part = jnp.einsum("rlp,lrv->vlp", leaf_basis, field_leaf, precision=precise)
    stacked = jnp.concatenate([vectors, coords], axis=0)
    window = with_halo(stacked, (("branch", 1),), leaves * leaf_size)
    window = window.reshape(vec_count + 2, leaves + 2 * leaves, leaf_size)
    own_leaves = stacked.reshape(vec_count + 2, leaves, leaf_size)
    source_group = near_list // (sub_count * leaves)
    source_local = near_list % leaves
    positions = leaves + (source_group - group_index) * leaves + source_local

    def near_block(block_start):
        chosen = lax.dynamic_slice_in_dim(positions, block_start, 4, 0)
        picked = jnp.take(window, chosen, axis=1)
        target = lax.dynamic_slice_in_dim(own_leaves, block_start, 4, 1)
        target_points = jnp.transpose(target[vec_count:], (1, 0, 2))[:, None]
        source_points = jnp.transpose(picked[vec_count:], (1, 2, 0, 3))
        kernel_tile = matern(target_points, source_points)
        return jnp.einsum("bjpq,vbjq->vbp", kernel_tile, picked[:vec_count], precision=precise)

    starts = jnp.arange(leaves // 4, dtype=jnp.int32) * 4
    near_part = lax.map(near_block, starts)
    near_part = jnp.transpose(near_part, (1, 0, 2, 3)).reshape(vec_count, leaves, leaf_size)
    product = near_part + far_part + NUGGET * leaf_vecs
    return product.reshape(vec_count, columns)


def solution(mesh):
    return jax.shard_map(
        body,
        mesh=mesh,
        in_specs=(
            P(None, ("branch", "sub")),
            P(None, ("branch", "sub")),
            P(None, ("branch", "sub")),
            P(("branch", "sub"), None, None),
            P(("branch", "sub"), None, None),
            P(("branch", "sub"), None, None),
            P(),
            P(("branch", "sub"), None),
            P(("branch", "sub"), None),
            P("branch", None),
        ),
        out_specs=P(None, ("branch", "sub")),
        check_vma=False,
    )
```

profile of v0, /device:TPU:8, one launch (start us, length us, event | category | flops | bytes accessed | tf_op | source)
XLA Modules:
  0.0 316.1 jit_solution(14932212776766272396)
XLA Ops:
  0.0 1.4 constant_dynamic-update-slice_fusion.1
  1.5 0.8 constant_dynamic-update-slice_fusion
  2.3 3.5 %collective-permute-start = (f32[66,4096]{1,0:T(8,128)S(1)}, f32[66,4096]{1,0:T(8,128)}, u32[]{:S(2)}, u32[]{:S(2)}) collective-permute-start(f32[66,4096]{1,0:T(8,128)S(1)} %constant_dynamic-update-slice_fusion), channel_id=1, source_target_pairs={{0,8},{8,16},{16,24},{24,32},{32,40},{40,48},{48,56},{56,64},{64,7... | collective-permute-start | bytes 3244040 | tf_op jit(solution)/shard_map/ppermute | solution.py:19
  5.8 6.6 %collective-permute-start.1 = (f32[66,4096]{1,0:T(8,128)S(1)}, f32[66,4096]{1,0:T(8,128)}, u32[]{:S(2)}, u32[]{:S(2)}) collective-permute-start(f32[66,4096]{1,0:T(8,128)S(1)} %constant_dynamic-update-slice_fusion), channel_id=1, source_target_pairs={{8,0},{16,8},{24,16},{32,24},{40,32},{48,40},{56,48},{64,56},{72,6... | collective-permute-start | bytes 3244040 | tf_op jit(solution)/shard_map/ppermute | solution.py:21
  12.3 73.9 %all_gather.9 = f32[64,2,32]{2,1,0:T(2,128)S(1)} all-gather(f32[1,2,32]{2,1,0:T(2,128)} %param.17), channel_id=1, replica_groups=mesh['branch'=64,'sub'=8] {'branch'}, dimensions={0}, use_global_device_ids=true | all-gather | bytes 16640 | tf_op jit(solution)/shard_map/all_gather | solution.py:76
  86.2 1.3 slice_bitcast_fusion.8
  87.5 1.7 fusion.36
  89.2 1.0 fusion.111
  90.4 23.6 %psum.7 = f32[1,32,64]{2,1,0:T(8,128)S(1)} all-reduce(f32[1,32,64]{2,1,0:T(8,128)S(1)} %convolution_bitcast_fusion.4), channel_id=1, replica_groups=mesh['branch'=64,'sub'=8] {'sub'}, use_global_device_ids=true, to_apply=%region_2.3 | all-reduce | flops 2048 | bytes 16384 | tf_op jit(solution)/shard_map/psum | solution.py:80
  114.0 47.4 %all_gather.11 = f32[64,32,64]{2,1,0:T(8,128)S(1)} all-gather(f32[1,32,64]{2,1,0:T(8,128)S(1)} %psum.7), channel_id=1, replica_groups=mesh['branch'=64,'sub'=8] {'branch'}, dimensions={0}, use_global_device_ids=true | all-gather | bytes 532480 | tf_op jit(solution)/shard_map/all_gather | solution.py:84
  161.4 1.1 fusion.38
  162.6 49.5 %all-gather = f32[2048,64]{1,0:T(8,128)S(1)} all-gather(f32[32,64]{1,0:T(8,128)S(1)} %bitcast.161), channel_id=2, replica_groups=mesh['branch'=64,'sub'=8] {'branch'}, dimensions={0}, use_global_device_ids=true | all-gather | bytes 532480 | tf_op jit(solution)/shard_map/all_gather | solution.py:77
  212.1 0.7 and_select_fusion
  213.2 1.1 slice.70
  215.0 1.1 fusion.40
  216.7 1.4 convolution_bitcast_fusion.1
  218.0 1.9 pad_maximum_fusion
  219.9 0.6 copy.77
  220.8 3.6 %copy.60 = f32[66,96,128]{2,0,1:T(8,128)} copy(f32[66,96,128]{2,1,0:T(8,128)S(1)} %slice.69) | data formatting | bytes 6488064 | tf_op jit(solution)/shard_map/while | solution.py:110
  224.4 87.0 %while.10 = (s32[]{:T(128)}, f32[8,64,4,128]{3,1,2,0:T(8,128)}, s32[8]{0:T(128)S(1)}, s32[32,9]{1,0:T(8,128)S(1)}, f32[66,96,128]{2,0,1:T(8,128)}, /*index=5*/f3...) while((s32[]{:T(128)}, f32[8,64,4,128]{3,1,2,0:T(8,128)}, s32[8]{0:T(128)S(1)}, ...), condition=%wide.region_1.2_spmd, body=%wide.region_0.1_spmd.sunk | while | flops 458598624 | bytes 6563411 | solution.py:110
  224.4 0.6 dynamic_slice.18
  226.8 2.6 gather_fusion
  229.7 0.7 dynamic-slice_bitcast_fusion.2
  230.5 4.8 %fusion.130 = f32[8,64,4,128]{3,1,2,0:T(8,128)} fusion(f32[8,64,4,128]{3,1,2,0:T(8,128)} %get-tuple-element.142, s32[]{:T(128)} %get-tuple-element.141, f32[4,9,128]{2,1,0:T(8,128)S(1)} %copy.110, f32[4,128]{1,0:T(4,128)S(1)} %get-tuple-element.128, f32[4,9,128]{2,1,0:T(8,128)S(1)} %copy.111, f32[4,128]{1,0:T(4,128)S(1)} %get-tuple-element.130, ...), kind=kOutput, calls=%fused_computation.22.clone.1 | convolution fusion | flops 458293248 | bytes 1380864 | tf_op jit(solution)/shard_map/while/body/eval_jaxpr/bjpq,vbjq->vbp/dot_general | solution.py:107
  235.3 0.6 dynamic_slice.18
  237.7 2.6 gather_fusion
  240.6 0.7 dynamic-slice_bitcast_fusion.2
  241.4 4.8 %fusion.130 = f32[8,64,4,128]{3,1,2,0:T(8,128)} fusion(f32[8,64,4,128]{3,1,2,0:T(8,128)} %get-tuple-element.142, s32[]{:T(128)} %get-tuple-element.141, f32[4,9,128]{2,1,0:T(8,128)S(1)} %copy.110, f32[4,128]{1,0:T(4,128)S(1)} %get-tuple-element.128, f32[4,9,128]{2,1,0:T(8,128)S(1)} %copy.111, f32[4,128]{1,0:T(4,128)S(1)} %get-tuple-element.130, ...), kind=kOutput, calls=%fused_computation.22.clone.1 | convolution fusion | flops 458293248 | bytes 1380864 | tf_op jit(solution)/shard_map/while/body/eval_jaxpr/bjpq,vbjq->vbp/dot_general | solution.py:107
  248.6 2.6 gather_fusion
  251.5 0.7 dynamic-slice_bitcast_fusion.2
  252.2 4.8 %fusion.130 = f32[8,64,4,128]{3,1,2,0:T(8,128)} fusion(f32[8,64,4,128]{3,1,2,0:T(8,128)} %get-tuple-element.142, s32[]{:T(128)} %get-tuple-element.141, f32[4,9,128]{2,1,0:T(8,128)S(1)} %copy.110, f32[4,128]{1,0:T(4,128)S(1)} %get-tuple-element.128, f32[4,9,128]{2,1,0:T(8,128)S(1)} %copy.111, f32[4,128]{1,0:T(4,128)S(1)} %get-tuple-element.130, ...), kind=kOutput, calls=%fused_computation.22.clone.1 | convolution fusion | flops 458293248 | bytes 1380864 | tf_op jit(solution)/shard_map/while/body/eval_jaxpr/bjpq,vbjq->vbp/dot_general | solution.py:107
  259.5 2.6 gather_fusion
  262.4 0.7 dynamic-slice_bitcast_fusion.2
  263.1 4.8 %fusion.130 = f32[8,64,4,128]{3,1,2,0:T(8,128)} fusion(f32[8,64,4,128]{3,1,2,0:T(8,128)} %get-tuple-element.142, s32[]{:T(128)} %get-tuple-element.141, f32[4,9,128]{2,1,0:T(8,128)S(1)} %copy.110, f32[4,128]{1,0:T(4,128)S(1)} %get-tuple-element.128, f32[4,9,128]{2,1,0:T(8,128)S(1)} %copy.111, f32[4,128]{1,0:T(4,128)S(1)} %get-tuple-element.130, ...), kind=kOutput, calls=%fused_computation.22.clone.1 | convolution fusion | flops 458293248 | bytes 1380864 | tf_op jit(solution)/shard_map/while/body/eval_jaxpr/bjpq,vbjq->vbp/dot_general | solution.py:107
  270.4 2.6 gather_fusion
  273.3 0.7 dynamic-slice_bitcast_fusion.2
  274.0 4.8 %fusion.130 = f32[8,64,4,128]{3,1,2,0:T(8,128)} fusion(f32[8,64,4,128]{3,1,2,0:T(8,128)} %get-tuple-element.142, s32[]{:T(128)} %get-tuple-element.141, f32[4,9,128]{2,1,0:T(8,128)S(1)} %copy.110, f32[4,128]{1,0:T(4,128)S(1)} %get-tuple-element.128, f32[4,9,128]{2,1,0:T(8,128)S(1)} %copy.111, f32[4,128]{1,0:T(4,128)S(1)} %get-tuple-element.130, ...), kind=kOutput, calls=%fused_computation.22.clone.1 | convolution fusion | flops 458293248 | bytes 1380864 | tf_op jit(solution)/shard_map/while/body/eval_jaxpr/bjpq,vbjq->vbp/dot_general | solution.py:107
  281.2 2.6 gather_fusion
  284.1 0.7 dynamic-slice_bitcast_fusion.2
  284.9 4.8 %fusion.130 = f32[8,64,4,128]{3,1,2,0:T(8,128)} fusion(f32[8,64,4,128]{3,1,2,0:T(8,128)} %get-tuple-element.142, s32[]{:T(128)} %get-tuple-element.141, f32[4,9,128]{2,1,0:T(8,128)S(1)} %copy.110, f32[4,128]{1,0:T(4,128)S(1)} %get-tuple-element.128, f32[4,9,128]{2,1,0:T(8,128)S(1)} %copy.111, f32[4,128]{1,0:T(4,128)S(1)} %get-tuple-element.130, ...), kind=kOutput, calls=%fused_computation.22.clone.1 | convolution fusion | flops 458293248 | bytes 1380864 | tf_op jit(solution)/shard_map/while/body/eval_jaxpr/bjpq,vbjq->vbp/dot_general | solution.py:107
  292.1 2.6 gather_fusion
  295.0 0.7 dynamic-slice_bitcast_fusion.2
  295.7 4.8 %fusion.130 = f32[8,64,4,128]{3,1,2,0:T(8,128)} fusion(f32[8,64,4,128]{3,1,2,0:T(8,128)} %get-tuple-element.142, s32[]{:T(128)} %get-tuple-element.141, f32[4,9,128]{2,1,0:T(8,128)S(1)} %copy.110, f32[4,128]{1,0:T(4,128)S(1)} %get-tuple-element.128, f32[4,9,128]{2,1,0:T(8,128)S(1)} %copy.111, f32[4,128]{1,0:T(4,128)S(1)} %get-tuple-element.130, ...), kind=kOutput, calls=%fused_computation.22.clone.1 | convolution fusion | flops 458293248 | bytes 1380864 | tf_op jit(solution)/shard_map/while/body/eval_jaxpr/bjpq,vbjq->vbp/dot_general | solution.py:107
  303.0 2.6 gather_fusion
  305.9 0.7 dynamic-slice_bitcast_fusion.2
  306.6 4.8 %fusion.130 = f32[8,64,4,128]{3,1,2,0:T(8,128)} fusion(f32[8,64,4,128]{3,1,2,0:T(8,128)} %get-tuple-element.142, s32[]{:T(128)} %get-tuple-element.141, f32[4,9,128]{2,1,0:T(8,128)S(1)} %copy.110, f32[4,128]{1,0:T(4,128)S(1)} %get-tuple-element.128, f32[4,9,128]{2,1,0:T(8,128)S(1)} %copy.111, f32[4,128]{1,0:T(4,128)S(1)} %get-tuple-element.130, ...), kind=kOutput, calls=%fused_computation.22.clone.1 | convolution fusion | flops 458293248 | bytes 1380864 | tf_op jit(solution)/shard_map/while/body/eval_jaxpr/bjpq,vbjq->vbp/dot_general | solution.py:107
  311.4 3.6 %fusion.33 = f32[32,8,8,128]{3,2,1,0:T(8,128)S(1)} fusion(f32[64,32,128]{2,0,1:T(8,128)} %bitcast.160, f32[32,32,64]{2,1,0:T(8,128)} %convolution_bitcast_fusion.1, f32[64,4096]{1,0:T(8,128)} %param.12, f32[32,4096]{1,0:T(8,128)S(1)} %copy-done), kind=kOutput, calls=%fused_computation.38 | convolution fusion | flops 101449728 | bytes 3932160 | tf_op jit(solution)/shard_map/rlp,lrv->vlp/dot_general | solution.py:91
  315.1 1.0 copy.105
  (119 shorter events, 8.5 us)
Async XLA Ops:
  0.0 87.5 %copy-start = (f32[32,4096]{1,0:T(8,128)S(1)}, f32[32,4096]{1,0:T(8,128)}, u32[]{:S(2)}) copy-start(f32[32,4096]{1,0:T(8,128)} %param.14) | copy-start | bytes 1572868
  0.0 87.5 %copy-start.1 = (f32[64,4096]{1,0:T(8,128)S(1)}, f32[64,4096]{1,0:T(8,128)}, u32[]{:S(2)}) copy-start(f32[64,4096]{1,0:T(8,128)} %param.12) | copy-start | bytes 3145732
  0.0 89.2 %copy-start.2 = (f32[32,32,32]{2,1,0:T(8,128)S(1)}, f32[32,32,32]{2,1,0:T(8,128)}, u32[]{:S(2)}) copy-start(f32[32,32,32]{2,1,0:T(8,128)} %param.15) | copy-start | bytes 393220
  0.0 90.2 %copy-start.4 = (f32[1,32,32]{2,1,0:T(8,128)S(1)}, f32[1,32,32]{2,1,0:T(8,128)}, u32[]{:S(2)}) copy-start(f32[1,32,32]{2,1,0:T(8,128)} %param.16) | copy-start | bytes 12292
  1.5 159.9 %copy-start.6 = (s32[1,8]{1,0:T(1,128)S(1)}, s32[1,8]{1,0:T(1,128)}, u32[]{:S(2)}) copy-start(s32[1,8]{1,0:T(1,128)} %param.21) | copy-start | bytes 100
  2.3 215.8 %collective-permute-start = (f32[66,4096]{1,0:T(8,128)S(1)}, f32[66,4096]{1,0:T(8,128)}, u32[]{:S(2)}, u32[]{:S(2)}) collective-permute-start(f32[66,4096]{1,0:T(8,128)S(1)} %constant_dynamic-update-slice_fusion), channel_id=1, source_target_pairs={{0,8},{8,16},{16,24},{24,32},{32,40},{40,48},{48,56},{56,64},{64,7... | collective-permute-start | bytes 3244040 | tf_op jit(solution)/shard_map/ppermute | solution.py:19
  5.8 212.3 %collective-permute-start.1 = (f32[66,4096]{1,0:T(8,128)S(1)}, f32[66,4096]{1,0:T(8,128)}, u32[]{:S(2)}, u32[]{:S(2)}) collective-permute-start(f32[66,4096]{1,0:T(8,128)S(1)} %constant_dynamic-update-slice_fusion), channel_id=1, source_target_pairs={{8,0},{16,8},{24,16},{32,24},{40,32},{48,40},{56,48},{64,56},{72,6... | collective-permute-start | bytes 3244040 | tf_op jit(solution)/shard_map/ppermute | solution.py:21
  87.5 75.0 %copy-start.3 = (f32[64,2,32]{0,2,1:T(8,128)S(1)}, f32[64,2,32]{0,2,1:T(8,128)}, u32[]{:S(2)}) copy-start(f32[64,2,32]{0,2,1:T(8,128)} %param.18) | copy-start | bytes 49156
  212.1 2.2 copy-start.5
  213.2 2.9 copy-start.7
where the time goes:
time: 317 us; the launch traced here: 316 us
  blocking collectives  194 us (61%)
  matrix products  49.8 us (16%)
  local copies, waits for them, and re-layouts  43.4 us (14%)
  loops' own time  14.3 us (5%)
  starting transfers between devices  10 us (3%)
  other arithmetic  4.03 us (1%)
    all_gather x1, blocking collectives, body(): lax.all_gather(skel_one, 'branch', axis=0, tiled=True)  73.9 us
    all_gather x1, blocking collectives, body(): lax.all_gather(coeff_node[None], 'branch', axis=0, tiled=True)  49.5 us
    all_gather x1, blocking collectives, body(): lax.all_gather(coeff_group[None], 'branch', axis=0, tiled=True)  47.4 us
    dot_general x8, matrix products, near_block(): jnp.einsum('bjpq,vbjq->vbp', kernel_tile, picked[:vec_count], precision=p...  38.5 us
    psum x1, blocking collectives, body(): coeff_group = lax.psum(upward, 'sub')  23.6 us
    gather x8, local copies, waits for them, and re-layouts, near_block(): picked = jnp.take(window, chosen, axis=1)  21.1 us
    another operation x1, loops' own time, body(): near_part = lax.map(near_block, starts)  14.3 us
    ppermute x1, starting transfers between devices, with_halo(): lax.ppermute(head, axis, [((i + 1) % count, i) for i in range(ends)])  6.55 us
  transfers between devices with their start and end apart: 2, of which 0 were waited for; matrix products, arithmetic and copies ran while one was open for 4% of the time, Pallas kernels for 0%

commit v1 on v0

v1 whole, which is shorter than its diff:
```python
import functools
import math

import jax
import jax.numpy as jnp
from jax import lax
from jax.experimental import pallas as pl
from jax.experimental.pallas import tpu as pltpu
from jax.sharding import PartitionSpec as P

MESH = pl.DeviceIdType.MESH
F32 = jnp.float32
BF16 = jnp.bfloat16
NUGGET = 0.5
LOG2E = math.log2(math.e)
LN2 = math.log(2.0)
SCALE = math.sqrt(3.0) / 0.7 * LOG2E
Y_COUNT = 8
LEAF = 128
RANK = 32
NV = 64
RIM = 8
UNROLL = 4
PAIRS = ((0, 1), (2, 3), (4, 5), (6, 7), (8,))
EXACT = lax.Precision.HIGHEST


def split(x):
    high = x.astype(BF16)
    return high, (x - high.astype(F32)).astype(BF16)


def matern_scaled(sx, sy, tx, ty):
    dx = sx - tx
    dy = sy - ty
    square = jnp.maximum(dx * dx + dy * dy, 1e-30)
    dist = square * lax.rsqrt(square)
    return (dist + LOG2E) * jnp.exp2(-dist)


def dot_f32(a, b, dims=((1,), (0,))):
    return lax.dot_general(a, b, (dims, ((), ())), precision=EXACT, preferred_element_type=F32)


def dot_bf16(a, b, dims=((1,), (0,))):
    return lax.dot_general(a, b, (dims, ((), ())), preferred_element_type=F32)


def fold(r):
    half = r.shape[0] // 2, r.shape[1] // 2
    return r[: half[0], : half[1]] + r[half[0] :, : half[1]] + r[: half[0], half[1] :] + r[half[0] :, half[1] :]


def leaf_cols(i):
    return pl.ds(pl.multiple_of(i * LEAF, LEAF), LEAF)


def kernel(
    sizes, vec, crd, bas, ltr, ntr, sk1, sk2, near, list1, list2, out,
    hv, hc, vw, sbx, sby, w3, g0, g1, gg, ps, ru, fc, send, recv,
):
    n_branch, n_sub, n_y = sizes
    n_z = n_branch // n_y
    leaves = ltr.shape[0]
    rows = 16 // n_sub
    b = lax.axis_index("branch")
    s = lax.axis_index("sub")
    z = b // n_y
    y = b % n_y
    lower = (b + n_branch - 1) % n_branch
    upper = (b + 1) % n_branch

    def y_peer(d):
        return z * n_y + (y + d) % n_y, s

    def z_peer(d):
        return ((z + d) % n_z) * n_y + y, s

    def sub_peer(d):
        return b, (s + d) % n_sub

    def remote(src, dst, k, peer):
        return pltpu.make_async_remote_copy(
            src_ref=src, dst_ref=dst, send_sem=send.at[k], recv_sem=recv.at[k], device_id=peer, device_id_type=MESH
        )

    ys, zs, ss = range(1, n_y), range(1, n_z), range(1, n_sub)
    barrier = pltpu.get_barrier_semaphore()
    peers = [sub_peer(d) for d in ss] + [y_peer(d) for d in ys] + [z_peer(d) for d in zs] + [(lower, s), (upper, s)]
    for peer in peers:
        pl.semaphore_signal(barrier, inc=1, device_id=peer, device_id_type=MESH)

    def own_vectors(i, c):
        high, low = split(vec[:, leaf_cols(i)] * LN2)
        vw[RIM + i, :NV] = high
        vw[RIM + i, NV:] = low
        return c

    lax.fori_loop(0, leaves, own_vectors, 0, unroll=4)
    pl.semaphore_wait(barrier, len(peers))

    rim = RIM * LEAF
    first, last = pl.ds(0, rim), pl.ds(leaves * LEAF - rim, rim)
    halo = [
        remote(crd.at[:, first], hc.at[1], 0, (lower, s)),
        remote(crd.at[:, last], hc.at[0], 1, (upper, s)),
        remote(vec.at[:, first], hv.at[1], 2, (lower, s)),
        remote(vec.at[:, last], hv.at[0], 3, (upper, s)),
    ]
    for copy in halo:
        copy.start()

    def make_w(i, c):
        cols = leaf_cols(i)
        bh, bl = split(bas[:, cols])
        lh, ll = split(ltr[i].T)
        w = dot_bf16(jnp.concatenate([lh, lh, ll], 1), jnp.concatenate([bh, bl, bh], 0))
        wh, wl = split(w)
        w3[:RANK, cols] = wh
        w3[RANK : 2 * RANK, cols] = wl
        w3[2 * RANK :, cols] = wh
        return c

    lax.fori_loop(0, leaves, make_w, 0, unroll=4)

    def up(i, c):
        return c + dot_bf16(vw[RIM + i], w3[: 2 * RANK, leaf_cols(i)], ((1,), (1,)))

    coeff_t = fold(lax.fori_loop(0, leaves, up, jnp.zeros((2 * NV, 2 * RANK), F32), unroll=4)) * (1.0 / LN2)
    up_t = dot_f32(coeff_t, ntr[0])
    packed = jnp.concatenate([up_t[16 * k : 16 * (k + 1)] for k in range(4)], 1)
    for p in range(n_sub):
        ps[p] = packed[p * rows : (p + 1) * rows]
    for d in ss:
        remote(ps.at[(s + d) % n_sub], ru.at[d], 8, sub_peer(d)).start()

    coeff = coeff_t.T
    g0[0, 0] = jnp.concatenate([coeff[0:8], coeff[8:16]], 1)
    g1[0, 0] = jnp.concatenate([coeff[16:24], coeff[24:32]], 1)
    gg[0, 0, rows : rows + 1] = jnp.concatenate([sk1[0, 0:1], sk1[0, 1:2], jnp.zeros((1, 2 * RANK), F32)], 1)
    for d in ys:
        remote(g0.at[0, 0], g0.at[0, d], 4, y_peer(d)).start()
    for d in zs:
        remote(g1.at[0, 0], g1.at[0, d], 5, z_peer(d)).start()

    def place_coords(i, row_x, row_y):
        sbx[i] = jnp.broadcast_to(row_x * SCALE, (LEAF, LEAF)).T
        sby[i] = jnp.broadcast_to(row_y * SCALE, (LEAF, LEAF)).T

    def own_coords(i, c):
        place_coords(RIM + i, crd[0:1, leaf_cols(i)], crd[1:2, leaf_cols(i)])
        return c

    lax.fori_loop(0, leaves, own_coords, 0, unroll=2)

    remote(ru.at[pl.ds(1, n_sub - 1)], ru.at[pl.ds(1, n_sub - 1)], 8, sub_peer(1)).wait_recv()
    total = ps[s]
    for d in ss:
        total = total + ru[d]
    gg[0, 0, 0:rows] = total
    for d in ys:
        remote(gg.at[0, 0], gg.at[0, d], 9, y_peer(d)).start()

    for copy in halo[:2]:
        copy.wait_recv()
    for side in range(2):
        base = side * (RIM + leaves)

        def rim_coords(i, c, side=side, base=base):
            place_coords(base + i, hc[side, 0:1, leaf_cols(i)], hc[side, 1:2, leaf_cols(i)])
            return c

        lax.fori_loop(0, RIM, rim_coords, 0, unroll=2)
    for copy in halo[2:]:
        copy.wait_recv()
    for side in range(2):
        base = side * (RIM + leaves)

        def rim_vectors(i, c, side=side, base=base):
            high, low = split(hv[side, :, leaf_cols(i)] * LN2)
            vw[base + i, :NV] = high
            vw[base + i, NV:] = low
            return c

        lax.fori_loop(0, RIM, rim_vectors, 0, unroll=4)

    def near_leaf(i):
        cols = leaf_cols(i)
        tx, ty = crd[0:1, cols] * SCALE, crd[1:2, cols] * SCALE
        slots = []
        for j in range(9):
            named = near[i, j]
            slot = (named // (n_sub * leaves) - b) * leaves + named % leaves + RIM
            slots.append(jnp.clip(slot, 0, leaves + 2 * RIM - 1))
        acc = None
        for pair in PAIRS:
            tiles = [
                jnp.concatenate(split(matern_scaled(sbx[slots[j]], sby[slots[j]], tx, ty)), 1) for j in pair
            ]
            part = dot_bf16(jnp.concatenate([vw[slots[j]] for j in pair], 1), jnp.concatenate(tiles, 0))
            acc = part if acc is None else acc + part
        out[:, cols] = fold(acc) + NUGGET * vec[:, cols]

    def forward():
        remote(gg.at[0, pl.ds(1, n_y - 1)], gg.at[0, pl.ds(1, n_y - 1)], 9, y_peer(1)).wait_recv()
        for d in zs:
            remote(gg.at[0], gg.at[d], 10, z_peer(d)).start()
        remote(g0.at[0, pl.ds(1, n_y - 1)], g0.at[0, pl.ds(1, n_y - 1)], 4, y_peer(1)).wait_recv()
        for d in zs:
            remote(g0.at[0], g0.at[d], 6, z_peer(d)).start()
        remote(g1.at[0, pl.ds(1, n_z - 1)], g1.at[0, pl.ds(1, n_z - 1)], 5, z_peer(1)).wait_recv()
        for d in ys:
            remote(g1.at[0], g1.at[d], 7, y_peer(d)).start()

    def place_of(branch):
        return (z + n_z - branch // n_y) % n_z, (y + n_y - branch % n_y) % n_y

    def far_tile(target, sources):
        column = (target * SCALE).T
        sx = jnp.concatenate([a for a, _ in sources], 1) * SCALE
        sy = jnp.concatenate([c for _, c in sources], 1) * SCALE
        wide = (RANK, sx.shape[1])
        return matern_scaled(
            jnp.broadcast_to(sx, wide), jnp.broadcast_to(sy, wide),
            jnp.broadcast_to(column[:, 0:1], wide), jnp.broadcast_to(column[:, 1:2], wide),
        ) * LN2

    def group_field():
        remote(gg.at[pl.ds(1, n_z - 1)], gg.at[pl.ds(1, n_z - 1)], 10, z_peer(1)).wait_recv()
        sources, coeffs = [], []
        for k in range(8):
            m = list2[0, k]
            dz, dy = place_of(m)
            skel = sk2[m]
            sources.append((skel[0:1], skel[1:2]))
            block = gg[dz, dy][0:rows]
            coeffs.append(jnp.concatenate([block[:, RANK * q : RANK * (q + 1)] for q in range(4)], 0))
        field = dot_f32(jnp.concatenate(coeffs, 1), far_tile(sk2[b], sources), ((1,), (1,)))
        fc[0] = jnp.concatenate([field[rows * q : rows * (q + 1)] for q in range(4)], 1)
        for d in ss:
            remote(fc.at[0], fc.at[d], 11, sub_peer(d)).start()

    def near_block(t, c):
        for u in range(UNROLL):
            near_leaf(t * UNROLL + u)

        @pl.when(t == 0)
        def _():
            forward()

        @pl.when(t == 2)
        def _():
            group_field()

        return c

    lax.fori_loop(0, leaves // UNROLL, near_block, 0)

    remote(g0.at[pl.ds(1, n_z - 1)], g0.at[pl.ds(1, n_z - 1)], 6, z_peer(1)).wait_recv()
    remote(g1.at[pl.ds(1, n_y - 1)], g1.at[pl.ds(1, n_y - 1)], 7, y_peer(1)).wait_recv()
    sources, coeffs = [], []
    for k in range(8):
        dz, dy = place_of(list1[0, k] // n_sub)
        skel = gg[dz, dy][rows : rows + 1]
        sources.append((skel[:, 0:RANK], skel[:, RANK : 2 * RANK]))
        for block in (g0[dz, dy], g1[dy, dz]):
            coeffs += [block[:, :NV], block[:, NV:]]
    field = dot_f32(far_tile(sk1[0], sources), jnp.concatenate(coeffs, 0))
    remote(fc.at[pl.ds(1, n_sub - 1)], fc.at[pl.ds(1, n_sub - 1)], 11, sub_peer(1)).wait_recv()
    packed = jnp.concatenate([fc[(s + n_sub - p) % n_sub] for p in range(n_sub)], 0)
    group_t = jnp.concatenate([packed[:, RANK * q : RANK * (q + 1)] for q in range(4)], 0)
    field = field + dot_f32(ntr[0], group_t, ((1,), (1,)))
    fh, fl = split(field.T)
    lhs = jnp.concatenate([fh, fh, fl], 1)

    def far(i, c):
        cols = pl.ds(pl.multiple_of(i * 2 * LEAF, 2 * LEAF), 2 * LEAF)
        out[:, cols] += dot_bf16(lhs, w3[:, cols])
        return c

    lax.fori_loop(0, leaves // 2, far, 0, unroll=4)

    for copy in halo:
        copy.wait_send()
    ny1, nz1, ns1 = pl.ds(1, n_y - 1), pl.ds(1, n_z - 1), pl.ds(1, n_sub - 1)
    for ref, k in (
        (g0.at[0, ny1], 4), (g1.at[0, nz1], 5), (g0.at[nz1], 6), (g1.at[ny1], 7),
        (ru.at[ns1], 8), (gg.at[0, ny1], 9), (gg.at[nz1], 10), (fc.at[ns1], 11),
    ):
        remote(ref, ref, k, sub_peer(1)).wait_send()


def body(sizes, vectors, coords, basis, leaf_transfer, node_transfer, skel_one, skel_two, near_list, list_one, list_two):
    n_branch, n_sub, n_y = sizes
    n_z = n_branch // n_y
    leaves = leaf_transfer.shape[0]
    window = leaves + 2 * RIM
    rows = 16 // n_sub
    rim = RIM * LEAF
    vmem = pl.BlockSpec(memory_space=pltpu.VMEM)
    smem = pl.BlockSpec(memory_space=pltpu.SMEM)
    return pl.pallas_call(
        functools.partial(kernel, sizes),
        out_shape=jax.ShapeDtypeStruct(vectors.shape, F32),
        in_specs=[vmem] * 7 + [smem] * 3,
        out_specs=vmem,
        scratch_shapes=[
            pltpu.VMEM((2, NV, rim), F32),
            pltpu.VMEM((2, 2, rim), F32),
            pltpu.VMEM((window, 2 * NV, LEAF), BF16),
            pltpu.VMEM((window, LEAF, LEAF), F32),
            pltpu.VMEM((window, LEAF, LEAF), F32),
            pltpu.VMEM((3 * RANK, leaves * LEAF), BF16),
            pltpu.VMEM((n_z, n_y, 8, 128), F32),
            pltpu.VMEM((n_y, n_z, 8, 128), F32),
            pltpu.VMEM((n_z, n_y, 2 * rows, 128), F32),
            pltpu.VMEM((n_sub, rows, 128), F32),
            pltpu.VMEM((n_sub, rows, 128), F32),
            pltpu.VMEM((n_sub, rows, 128), F32),
            pltpu.SemaphoreType.DMA((12,)),
            pltpu.SemaphoreType.DMA((12,)),
        ],
        compiler_params=pltpu.CompilerParams(
            collective_id=0, has_side_effects=True, vmem_limit_bytes=48 * 2**20
        ),
        name="h2_product",
    )(vectors, coords, basis, leaf_transfer, node_transfer, skel_one, skel_two, near_list, list_one, list_two)


def solution(mesh, y_count=Y_COUNT):
    both = ("branch", "sub")
    return jax.shard_map(
        functools.partial(body, (mesh.shape["branch"], mesh.shape["sub"], y_count)),
        mesh=mesh,
        in_specs=(
            P(None, both),
            P(None, both),
            P(None, both),
            P(both, None, None),
            P(both, None, None),
            P(both, None, None),
            P(),
            P(both, None),
            P(both, None),
            P("branch", None),
        ),
        out_specs=P(None, both),
        check_vma=False,
    )
```

time: 317 us -> 49.1 us (0.15)
  the two profiles are of different devices: /device:TPU:8 before, /device:TPU:2 now
where the time goes in v1:
time: 49.1 us; the launch traced here: 48.8 us
  Pallas kernels  42.7 us (87%)
  local copies, waits for them, and re-layouts  5.97 us (12%)
    pallas_call x1, Pallas kernels, body(): pl.pallas_call(functools.partial(kernel, sizes), out_shape=jax.ShapeDtype...  42.7 us
    unnamed x19, local copies, waits for them, and re-layouts  5.97 us

profile of v1, /device:TPU:2, one launch (start us, length us, event | category | flops | bytes accessed | tf_op | source)
XLA Modules:
  0.0 48.8 jit_solution(17045815255099489793)
XLA Ops:
  0.0 0.8 %copy.12.near = s32[32,9]{1,0:T(8,128)S(1)} copy(s32[32,9]{0,1:T(8,128)} %param.17) | data formatting | bytes 2304 | tf_op args[7]
  0.8 0.0 copy-start.3
  0.8 0.0 copy-start.4
  0.8 0.0 copy-start.5
  0.8 0.0 copy-start.6
  0.8 0.0 copy-start.7
  0.8 0.9 %copy.11.sk2 = f32[64,2,32]{2,1,0:T(2,128)S(1)} copy(f32[64,2,32]{0,2,1:T(8,128)} %param.16) | data formatting | bytes 32768 | tf_op args[6]
  1.7 0.0 copy-done.3
  1.7 0.0 copy-done.4
  1.7 0.0 copy-done.5
  1.7 0.0 copy-done.6
  1.7 0.0 copy-done.7
  1.8 0.0 copy-start
  1.8 1.2 %copy-done = f32[64,4096]{1,0:T(8,128)S(1)} copy-done((f32[64,4096]{1,0:T(8,128)S(1)}, f32[64,4096]{1,0:T(8,128)}, u32[]{:S(2)}) %copy-start) | copy-done | bytes 1048600
  3.0 0.0 copy-start.1
  3.0 1.0 %copy-done.1 = f32[32,4096]{1,0:T(8,128)S(1)} copy-done((f32[32,4096]{1,0:T(8,128)S(1)}, f32[32,4096]{1,0:T(8,128)}, u32[]{:S(2)}) %copy-start.1) | copy-done | bytes 524312
  4.0 0.0 copy-start.2
  4.0 1.0 %copy-done.2 = f32[32,32,32]{2,1,0:T(8,128)S(1)} copy-done((f32[32,32,32]{2,1,0:T(8,128)S(1)}, f32[32,32,32]{2,1,0:T(8,128)}, u32[]{:S(2)}) %copy-start.2) | copy-done | bytes 131096
  5.1 42.7 %h2_product.1 = f32[64,4096]{1,0:T(8,128)S(1)} custom-call(f32[64,4096]{1,0:T(8,128)S(1)} %copy-done, f32[2,4096]{1,0:T(2,128)S(1)} %copy-done.3, f32[32,4096]{1,0:T(8,128)S(1)} %copy-done.1, f32[32,32,32]{2,1,0:T(8,128)S(1)} %copy-done.2, f32[1,32,32]{2,1,0:T(8,128)S(1)} %copy-done.4, f32[1,2,32]{2,1,0:T(2,128)S(1)} %copy-done.5, ...), custom_call_target="tpu_custom_call" | custom-call | tf_op jit(solution)/shard_map/h2_product/pallas_call | solution.py:302
  47.8 1.0 %copy.14 = f32[64,4096]{1,0:T(8,128)} copy(f32[64,4096]{1,0:T(8,128)S(1)} %h2_product.1) | data formatting | bytes 2097152
Async XLA Ops:
  0.8 0.9 %copy-start.3 = (f32[2,4096]{1,0:T(2,128)S(1)}, f32[2,4096]{1,0:T(2,128)}, u32[]{:S(2)}) copy-start(f32[2,4096]{1,0:T(2,128)} %crd.1) | copy-start | bytes 98308
  0.8 0.9 %copy-start.4 = (f32[1,32,32]{2,1,0:T(8,128)S(1)}, f32[1,32,32]{2,1,0:T(8,128)}, u32[]{:S(2)}) copy-start(f32[1,32,32]{2,1,0:T(8,128)} %ntr.1) | copy-start | bytes 12292
  0.8 0.9 %copy-start.5 = (f32[1,2,32]{2,1,0:T(2,128)S(1)}, f32[1,2,32]{2,1,0:T(2,128)}, u32[]{:S(2)}) copy-start(f32[1,2,32]{2,1,0:T(2,128)} %sk1.1) | copy-start | bytes 772
  0.8 1.0 %copy-start.6 = (s32[1,8]{1,0:T(1,128)S(1)}, s32[1,8]{1,0:T(1,128)}, u32[]{:S(2)}) copy-start(s32[1,8]{1,0:T(1,128)} %list1.1) | copy-start | bytes 100
  0.8 1.0 %copy-start.7 = (s32[1,8]{1,0:T(1,128)S(1)}, s32[1,8]{1,0:T(1,128)}, u32[]{:S(2)}) copy-start(s32[1,8]{1,0:T(1,128)} %list2.1) | copy-start | bytes 100
  1.8 1.2 %copy-start = (f32[64,4096]{1,0:T(8,128)S(1)}, f32[64,4096]{1,0:T(8,128)}, u32[]{:S(2)}) copy-start(f32[64,4096]{1,0:T(8,128)} %vec.1) | copy-start | bytes 3145732
  3.0 1.0 %copy-start.1 = (f32[32,4096]{1,0:T(8,128)S(1)}, f32[32,4096]{1,0:T(8,128)}, u32[]{:S(2)}) copy-start(f32[32,4096]{1,0:T(8,128)} %bas.1) | copy-start | bytes 1572868
  4.0 1.0 %copy-start.2 = (f32[32,32,32]{2,1,0:T(8,128)S(1)}, f32[32,32,32]{2,1,0:T(8,128)}, u32[]{:S(2)}) copy-start(f32[32,32,32]{2,1,0:T(8,128)} %ltr.1) | copy-start | bytes 393220

commit v2 on v1

v2 whole, which is shorter than its diff:
```python
import functools
import math

import jax
import jax.numpy as jnp
from jax import lax
from jax.experimental import pallas as pl
from jax.experimental.pallas import tpu as pltpu
from jax.sharding import PartitionSpec as P

MESH = pl.DeviceIdType.MESH
F32 = jnp.float32
BF16 = jnp.bfloat16
NUGGET = 0.5
LOG2E = math.log2(math.e)
LN2 = math.log(2.0)
SCALE = math.sqrt(3.0) / 0.7 * LOG2E
Y_COUNT = 8
LEAF = 128
RANK = 32
NV = 64
RIM = 8
BLOCK = 8
PAIRS = ((0, 1), (2, 3), (4, 5), (6, 7), (8,))
EXACT = lax.Precision.HIGHEST
CENTRE = 1.5
VMEM_LIMIT = 62 * 2**20
FEATURES = 32
NN, NT, TN = ((1,), (0,)), ((1,), (1,)), ((0,), (0,))


def split(x):
    high = x.astype(BF16)
    return high, (x - high.astype(F32)).astype(BF16)


def split3(x):
    first = x.astype(BF16).astype(F32)
    rest = x - first
    second = rest.astype(BF16).astype(F32)
    return first, second, rest - second


def matern_of(square):
    square = jnp.maximum(square, 1e-30)
    dist = square * lax.rsqrt(square)
    return (dist + LOG2E) * jnp.exp2(-dist)


def features(coords):
    w = (coords - CENTRE) * SCALE
    norm = w[0:1] * w[0:1] + w[1:2] * w[1:2]
    s1, s2, s3 = split3(w)
    norms = split3(norm)
    ones = [jnp.ones_like(norm)] * 3
    zeros = jnp.zeros((FEATURES - 18, w.shape[1]), F32)
    t1, t2, t3 = -2.0 * s1, -2.0 * s2, -2.0 * s3
    source = jnp.concatenate([s1, s1, s2, s2, s1, s3, *norms, *ones, zeros], 0)
    target = jnp.concatenate([t1, t2, t1, t2, t3, t1, *ones, *norms, zeros], 0)
    return source, target


def dot_f32(a, b, dims=NN):
    return lax.dot_general(a, b, (dims, ((), ())), precision=EXACT, preferred_element_type=F32)


def dot_bf16(a, b, dims=NN):
    return lax.dot_general(a, b, (dims, ((), ())), preferred_element_type=F32)


def fold(r):
    half = r.shape[0] // 2, r.shape[1] // 2
    return r[: half[0], : half[1]] + r[half[0] :, : half[1]] + r[: half[0], half[1] :] + r[half[0] :, half[1] :]


def leaf_cols(i):
    return pl.ds(pl.multiple_of(i * LEAF, LEAF), LEAF)


def kernel(sizes, *refs):
    operands, out = refs[:10], refs[10]
    vec, crd, bas, ltr, ntr, sk1, sk2, near, list1, list2 = refs[11:21]
    hv, hc, vw, fs, ft, w3, sk2t, gy, gz, gs, ps, ru, fc, load, send, recv, later = refs[21:]
    n_branch, n_sub, n_y = sizes
    n_z = n_branch // n_y
    leaves = ltr.shape[0]
    rows = 16 // n_sub
    ny1, nz1, ns1 = pl.ds(1, n_y - 1), pl.ds(1, n_z - 1), pl.ds(1, n_sub - 1)
    b = lax.axis_index("branch")
    s = lax.axis_index("sub")
    z = b // n_y
    y = b % n_y

    loads = [pltpu.make_async_copy(operands[k], refs[11 + k], load.at[k]) for k in range(10)]
    l_vec, l_crd, l_bas, l_ltr, l_ntr, l_sk1, l_sk2, l_near, l_list1, l_list2 = loads
    for copy in (l_ltr, l_bas, l_vec, l_crd, l_ntr, l_sk1, l_sk2, l_near, l_list1, l_list2):
        copy.start()

    def y_peer(d):
        return z * n_y + (y + d) % n_y, s

    def z_peer(d):
        return ((z + d) % n_z) * n_y + y, s

    def sub_peer(d):
        return b, (s + d) % n_sub

    def remote(src, dst, k, peer):
        return pltpu.make_async_remote_copy(
            src_ref=src, dst_ref=dst, send_sem=send.at[k], recv_sem=recv.at[k], device_id=peer, device_id_type=MESH
        )

    def signal(sem, peer):
        pl.semaphore_signal(sem, inc=1, device_id=peer, device_id_type=MESH)

    ys, zs, ss = range(1, n_y), range(1, n_z), range(1, n_sub)
    has_lower, has_upper = b > 0, b < n_branch - 1
    lower, upper = (b - 1, s), (b + 1, s)

    barrier = pltpu.get_barrier_semaphore()
    pl.when(has_lower)(lambda: signal(barrier, lower))
    pl.when(has_upper)(lambda: signal(barrier, upper))
    for d in ss:
        signal(barrier, sub_peer(d))
    for d in ys:
        signal(barrier, y_peer(d))
    for other in range(1, n_z):
        pl.when(other > z)(lambda other=other: signal(barrier, (other * n_y + y, s)))

    for side, missing in ((0, b == 0), (1, b == n_branch - 1)):

        @pl.when(missing)
        def _(side=side):
            hv[side] = jnp.zeros(hv.shape[1:], F32)
            hc[side] = jnp.zeros(hc.shape[1:], F32)

    l_ltr.wait()
    l_bas.wait()

    def make_w(i, c):
        cols = leaf_cols(i)
        bh, bl = split(bas[:, cols])
        lh, ll = split(ltr[i])
        w = dot_bf16(jnp.concatenate([lh, lh, ll], 0), jnp.concatenate([bh, bl, bh], 0), TN)
        wh, wl = split(w)
        w3[:RANK, cols] = wh
        w3[RANK : 2 * RANK, cols] = wl
        w3[2 * RANK :, cols] = wh
        return c

    lax.fori_loop(0, leaves, make_w, 0, unroll=16)

    l_vec.wait()

    def own_vectors(i, c):
        high, low = split(vec[:, leaf_cols(i)] * LN2)
        vw[RIM + i, :NV] = high
        vw[RIM + i, NV:] = low
        return c

    lax.fori_loop(0, leaves, own_vectors, 0, unroll=8)
    own = jnp.concatenate([vw[RIM + i] for i in range(leaves)], 1)
    coeff_t = fold(dot_bf16(own, w3[: 2 * RANK], NT)) * (1.0 / LN2)
    l_ntr.wait()
    up_t = dot_f32(coeff_t, ntr[0])
    packed = jnp.concatenate([up_t[16 * k : 16 * (k + 1)] for k in range(4)], 1)
    for p in range(n_sub):
        ps[p] = packed[p * rows : (p + 1) * rows]

    met = n_sub - 1 + n_y - 1 + z + has_lower.astype(jnp.int32) + has_upper.astype(jnp.int32)
    pl.semaphore_wait(barrier, met)
    for d in ss:
        remote(ps.at[(s + d) % n_sub], ru.at[d], 8, sub_peer(d)).start()
    for other in range(n_z - 1):
        pl.when(other < z)(lambda other=other: signal(later, (other * n_y + y, s)))

    rim = RIM * LEAF
    first, last = pl.ds(0, rim), pl.ds(leaves * LEAF - rim, rim)
    down = [remote(crd.at[:, first], hc.at[1], 0, lower), remote(vec.at[:, first], hv.at[1], 2, lower)]
    up = [remote(crd.at[:, last], hc.at[0], 1, upper), remote(vec.at[:, last], hv.at[0], 3, upper)]

    def start_all(copies):
        for copy in copies:
            copy.start()

    def send_halo():
        pl.when(has_lower)(lambda: start_all(down))
        pl.when(has_upper)(lambda: start_all(up))

    coeff = coeff_t.T
    coeff = jnp.concatenate([coeff[:16], coeff[16:]], 1)
    for k in range(3):
        gy[0, 0, k] = coeff[4 * k : 4 * (k + 1)]
    gz[0, 0] = coeff[12:16]
    for d in ys:
        remote(gy.at[0, 0], gy.at[0, d], 4, y_peer(d)).start()

    l_crd.wait()
    send_halo()
    wide = 8 * LEAF

    def own_features(i, c):
        cols = pl.ds(pl.multiple_of(i * wide, wide), wide)
        source, target = features(crd[:, cols])
        ft[:, cols] = target.astype(BF16)
        flat = source.T.astype(BF16)
        for k in range(8):
            fs[RIM + i * 8 + k] = flat[k * LEAF : (k + 1) * LEAF]
        return c

    lax.fori_loop(0, leaves // 8, own_features, 0)
    l_sk1.wait()
    gs[0, 0, rows : rows + 1] = jnp.concatenate([sk1[0, 0:1], sk1[0, 1:2], jnp.zeros((1, 2 * RANK), F32)], 1)

    remote(ru.at[ns1], ru.at[ns1], 8, sub_peer(1)).wait_recv()
    total = ps[s]
    for d in ss:
        total = total + ru[d]
    gs[0, 0, 0:rows] = total

    @pl.when(z < n_z - 1)
    def _():
        pl.semaphore_wait(later, n_z - 1 - z)

    for d in zs:
        remote(gs.at[0, 0], gs.at[0, d], 11, z_peer(d)).start()
    for d in zs:
        remote(gz.at[0, 0], gz.at[0, d], 5, z_peer(d)).start()

    def pass_on():
        remote(gs.at[0, nz1], gs.at[0, nz1], 11, z_peer(1)).wait_recv()
        for d in ys:
            remote(gs.at[0], gs.at[d], 7, y_peer(d)).start()
        remote(gy.at[0, ny1], gy.at[0, ny1], 4, y_peer(1)).wait_recv()
        for d in zs:
            remote(gy.at[0], gy.at[d], 6, z_peer(d)).start()

    passes_first = b >= n_branch // 2 - 1
    pl.when(passes_first)(pass_on)
    l_sk2.wait()
    sk2t[...] = jnp.concatenate([sk2[0].T, sk2[1].T], 1)
    l_near.wait()
    l_list1.wait()
    l_list2.wait()

    def rims(wait_k, take):
        for side, there, copies in ((0, has_lower, up), (1, has_upper, down)):
            pl.when(there)(lambda copies=copies: copies[wait_k].wait_recv())
            take(side, side * (RIM + leaves))

    def rim_features(side, base):
        source, _ = features(hc[side])
        flat = source.T.astype(BF16)
        for k in range(RIM):
            fs[base + k] = flat[k * LEAF : (k + 1) * LEAF]

    def rim_vectors(side, base):
        for i in range(RIM):
            high, low = split(hv[side, :, i * LEAF : (i + 1) * LEAF] * LN2)
            vw[base + i, :NV] = high
            vw[base + i, NV:] = low

    rims(0, rim_features)
    rims(1, rim_vectors)

    def near_leaves(first_leaf):
        items = [(first_leaf + u, pair) for u in range(BLOCK) for pair in PAIRS]

        def slots(i, pair):
            found = []
            for j in pair:
                named = near[j, i]
                slot = (named // (n_sub * leaves) - b) * leaves + named % leaves + RIM
                found.append(jnp.clip(slot, 0, leaves + 2 * RIM - 1))
            return found

        squares, tiles, acc = {}, {}, None
        for step in range(len(items) + 2):
            if step < len(items):
                i, pair = items[step]
                named = slots(i, pair)
                sources = jnp.concatenate([fs[m] for m in named], 0)
                squares[step] = named, dot_bf16(sources, ft[:, leaf_cols(i)])
            if 0 <= step - 1 < len(items):
                named, square = squares.pop(step - 1)
                tiles[step - 1] = named, jnp.concatenate(split(matern_of(square)), 1)
            if step >= 2:
                i, pair = items[step - 2]
                named, tile = tiles.pop(step - 2)
                part = dot_bf16(jnp.concatenate([vw[m] for m in named], 1), tile)
                acc = part if acc is None else acc + part
                if pair == PAIRS[-1]:
                    out[:, leaf_cols(i)] = fold(acc) + NUGGET * vec[:, leaf_cols(i)]
                    acc = None

    def place_of(branch):
        return (z + n_z - branch // n_y) % n_z, (y + n_y - branch % n_y) % n_y

    def far_tile(target, sources):
        column = (jnp.concatenate([target[:, :RANK], target[:, RANK : 2 * RANK]], 0) * SCALE).T
        sx = jnp.concatenate([row[:, :RANK] for row in sources], 1) * SCALE
        sy = jnp.concatenate([row[:, RANK : 2 * RANK] for row in sources], 1) * SCALE
        dx = sx - column[:, 0:1]
        dy = sy - column[:, 1:2]
        return matern_of(dx * dx + dy * dy) * LN2

    def group_field():
        remote(gs.at[ny1], gs.at[ny1], 7, y_peer(1)).wait_recv()
        remote(gz.at[0, nz1], gz.at[0, nz1], 5, z_peer(1)).wait_recv()
        for d in ys:
            remote(gz.at[0], gz.at[d], 9, y_peer(d)).start()
        sources, coeffs = [], []
        for k in range(8):
            m = list2[0, k]
            dz, dy = place_of(m)
            sources.append(sk2t[pl.ds(m, 1)])
            block = gs[dy, dz][0:rows]
            coeffs.append(jnp.concatenate([block[:, RANK * q : RANK * (q + 1)] for q in range(4)], 0))
        field = dot_f32(jnp.concatenate(coeffs, 1), far_tile(sk2t[pl.ds(b, 1)], sources), NT)
        fc[0] = jnp.concatenate([field[rows * q : rows * (q + 1)] for q in range(4)], 1)
        for d in ss:
            remote(fc.at[0], fc.at[d], 10, sub_peer(d)).start()

    blocks = leaves // BLOCK
    pass_step = jnp.where(passes_first, blocks, jnp.where(z >= n_z // 4, 1, 2))
    group_step = jnp.where(z >= n_z // 2, 2, jnp.where(z >= n_z // 4, 3, blocks))

    def near_block(t, c):
        pl.when(t == pass_step)(pass_on)
        pl.when(t == group_step)(group_field)
        near_leaves(t * BLOCK)
        return c

    lax.fori_loop(0, blocks, near_block, 0)
    pl.when(group_step == blocks)(group_field)

    remote(gy.at[nz1], gy.at[nz1], 6, z_peer(1)).wait_recv()
    remote(gz.at[ny1], gz.at[ny1], 9, y_peer(1)).wait_recv()
    sources, coeffs = [], []
    for k in range(8):
        dz, dy = place_of(list1[0, k] // n_sub)
        sources.append(gs[dy, dz][rows : rows + 1])
        block = jnp.concatenate([gy[dz, dy, 0], gy[dz, dy, 1], gy[dz, dy, 2], gz[dy, dz]], 0)
        coeffs += [block[:, :NV], block[:, NV:]]
    field = dot_f32(far_tile(gs[0, 0][rows : rows + 1], sources), jnp.concatenate(coeffs, 0))
    remote(fc.at[ns1], fc.at[ns1], 10, sub_peer(1)).wait_recv()
    packed = jnp.concatenate([fc[(s + n_sub - p) % n_sub] for p in range(n_sub)], 0)
    group_t = jnp.concatenate([packed[:, RANK * q : RANK * (q + 1)] for q in range(4)], 0)
    field = field + dot_f32(ntr[0], group_t, NT)
    fh, fl = split(field.T)
    lhs = jnp.concatenate([fh, fh, fl], 1)

    def far(i, c):
        cols = pl.ds(pl.multiple_of(i * 2 * LEAF, 2 * LEAF), 2 * LEAF)
        out[:, cols] += dot_bf16(lhs, w3[:, cols])
        return c

    lax.fori_loop(0, leaves // 2, far, 0, unroll=8)

    def finish(copies):
        for copy in copies:
            copy.wait_send()

    pl.when(has_lower)(lambda: finish(down))
    pl.when(has_upper)(lambda: finish(up))
    for ref, k in (
        (gy.at[0, ny1], 4), (gz.at[0, nz1], 5), (gy.at[nz1], 6), (gs.at[ny1], 7),
        (ru.at[ns1], 8), (gz.at[ny1], 9), (fc.at[ns1], 10), (gs.at[0, nz1], 11),
    ):
        remote(ref, ref, k, sub_peer(1)).wait_send()


def body(sizes, vectors, coords, basis, leaf_transfer, node_transfer, skel_one, skel_two, near_list, list_one, list_two):
    n_branch, n_sub, n_y = sizes
    n_z = n_branch // n_y
    leaves = leaf_transfer.shape[0]
    window = leaves + 2 * RIM
    rows = 16 // n_sub
    rim = RIM * LEAF
    operands = (
        vectors, coords, basis, leaf_transfer, node_transfer, skel_one,
        jnp.transpose(skel_two, (1, 2, 0)), near_list.T, list_one, list_two,
    )
    held = [pltpu.VMEM(a.shape, F32) for a in operands[:7]] + [pltpu.SMEM(a.shape, jnp.int32) for a in operands[7:]]
    return pl.pallas_call(
        functools.partial(kernel, sizes),
        out_shape=jax.ShapeDtypeStruct(vectors.shape, F32),
        in_specs=[pl.BlockSpec(memory_space=pltpu.HBM)] * 10,
        out_specs=pl.BlockSpec(memory_space=pltpu.VMEM),
        scratch_shapes=[
            *held,
            pltpu.VMEM((2, NV, rim), F32),
            pltpu.VMEM((2, 2, rim), F32),
            pltpu.VMEM((window, 2 * NV, LEAF), BF16),
            pltpu.VMEM((window, LEAF, FEATURES), BF16),
            pltpu.VMEM((FEATURES, leaves * LEAF), BF16),
            pltpu.VMEM((3 * RANK, leaves * LEAF), BF16),
            pltpu.VMEM((n_branch, 2 * RANK), F32),
            pltpu.VMEM((n_z, n_y, 3, 4, 128), F32),
            pltpu.VMEM((n_y, n_z, 4, 128), F32),
            pltpu.VMEM((n_y, n_z, 2 * rows, 128), F32),
            pltpu.VMEM((n_sub, rows, 128), F32),
            pltpu.VMEM((n_sub, rows, 128), F32),
            pltpu.VMEM((n_sub, rows, 128), F32),
            pltpu.SemaphoreType.DMA((10,)),
            pltpu.SemaphoreType.DMA((12,)),
            pltpu.SemaphoreType.DMA((12,)),
            pltpu.SemaphoreType.REGULAR,
        ],
        compiler_params=pltpu.CompilerParams(
            collective_id=0, has_side_effects=True, vmem_limit_bytes=VMEM_LIMIT
        ),
        name="h2_product",
    )(*operands)


def solution(mesh, y_count=Y_COUNT):
    both = ("branch", "sub")
    return jax.shard_map(
        functools.partial(body, (mesh.shape["branch"], mesh.shape["sub"], y_count)),
        mesh=mesh,
        in_specs=(
            P(None, both),
            P(None, both),
            P(None, both),
            P(both, None, None),
            P(both, None, None),
            P(both, None, None),
            P(),
            P(both, None),
            P(both, None),
            P("branch", None),
        ),
        out_specs=P(None, both),
        check_vma=False,
    )
```

time: 49.1 us -> 40.3 us (0.82)
  the two profiles are of different devices: /device:TPU:2 before, /device:TPU:1 now
where the time goes in v2:
time: 40.3 us; the launch traced here: 39.6 us
  Pallas kernels  37.3 us (93%)
  local copies, waits for them, and re-layouts  2.27 us (6%)
    pallas_call x1, Pallas kernels, body(): pl.pallas_call(functools.partial(kernel, sizes), out_shape=jax.ShapeDtype...  37.3 us
    unnamed x1, local copies, waits for them, and re-layouts  2.27 us

profile of v2, /device:TPU:1, one launch (start us, length us, event | category | flops | bytes accessed | tf_op | source)
XLA Modules:
  0.0 39.6 jit_solution(15121902091691014981)
XLA Ops:
  0.0 37.3 %h2_product.1 = f32[64,4096]{1,0:T(8,128)} custom-call(f32[64,4096]{1,0:T(8,128)} %refs_0_.1, f32[2,4096]{1,0:T(2,128)} %refs_1_.1, f32[32,4096]{1,0:T(8,128)} %refs_2_.1, f32[32,32,32]{2,1,0:T(8,128)} %refs_3_.1, f32[1,32,32]{2,1,0:T(8,128)} %refs_4_.1, f32[1,2,32]{2,1,0:T(2,128)} %refs_5_.1, f32[2,32,64]{2,1,0:T(8,128)} %bitcast.2, s32[9,32]{1,0:T(8,128)} %bitcast.3, ...), custom_call_target="tpu_custom_call" | custom-call | tf_op jit(solution)/shard_map/h2_product/pallas_call | solution.py:385
  37.3 2.3 %copy.12 = f32[64,4096]{1,0:T(8,128)} copy(f32[64,4096]{1,0:T(8,128)} %h2_product.1) | data formatting | bytes 2097152

commit v3 on v2

--- a/solution.py
+++ b/solution.py
@@ -64,6 +64,10 @@
     return lax.dot_general(a, b, (dims, ((), ())), precision=EXACT, preferred_element_type=F32)
 
 
+def dot_high(a, b, dims=NN):
+    return lax.dot_general(a, b, (dims, ((), ())), precision=lax.Precision.HIGH, preferred_element_type=F32)
+
+
 def dot_bf16(a, b, dims=NN):
     return lax.dot_general(a, b, (dims, ((), ())), preferred_element_type=F32)
 
@@ -80,11 +84,10 @@
 def kernel(sizes, *refs):
     operands, out = refs[:10], refs[10]
     vec, crd, bas, ltr, ntr, sk1, sk2, near, list1, list2 = refs[11:21]
-    hv, hc, vw, fs, ft, w3, sk2t, gy, gz, gs, ps, ru, fc, load, send, recv, later = refs[21:]
+    hv, hc, vw, fs, ft, w3, sk2t, info, early, column, mix, part, parts, own_field, fc, load, send, recv, later = refs[21:]
     n_branch, n_sub, n_y = sizes
     n_z = n_branch // n_y
     leaves = ltr.shape[0]
-    rows = 16 // n_sub
     ny1, nz1, ns1 = pl.ds(1, n_y - 1), pl.ds(1, n_z - 1), pl.ds(1, n_sub - 1)
     b = lax.axis_index("branch")
     s = lax.axis_index("sub")
@@ -126,6 +129,34 @@
         signal(barrier, y_peer(d))
     for other in range(1, n_z):
         pl.when(other > z)(lambda other=other: signal(barrier, (other * n_y + y, s)))
+
+    starts_late = z >= n_z // 2
+    met = n_sub - 1 + n_y - 1 + z + has_lower.astype(jnp.int32) + has_upper.astype(jnp.int32)
+
+    def along_z(ref, k, higher):
+        for d in zs:
+            pl.when(z + d < n_z if higher else z + d >= n_z)(
+                lambda d=d: remote(ref.at[0], ref.at[d], k, z_peer(d)).start()
+            )
+
+    def enter():
+        pl.semaphore_wait(barrier, met)
+        for other in range(n_z - 1):
+            pl.when(other < z)(lambda other=other: signal(later, (other * n_y + y, s)))
+        l_sk1.wait()
+        l_list1.wait()
+        l_list2.wait()
+        l_ntr.wait()
+        row = [sk1[0, 0:1], sk1[0, 1:2], list1[...].astype(F32), list2[...].astype(F32)]
+        row = jnp.concatenate(row + [jnp.zeros((1, 128 - 2 * RANK - 16), F32)], 1)
+        info[0] = row
+        early[0, 8:9] = row
+        early[0, 0:8] = jnp.concatenate([ntr[0, 8 * k : 8 * (k + 1)] for k in range(4)], 1)
+        for d in ys:
+            remote(info.at[0], info.at[d], 4, y_peer(d)).start()
+        along_z(early, 8, False)
+
+    pl.when(starts_late)(enter)
 
     for side, missing in ((0, b == 0), (1, b == n_branch - 1)):
 
@@ -161,42 +192,37 @@
     lax.fori_loop(0, leaves, own_vectors, 0, unroll=8)
     own = jnp.concatenate([vw[RIM + i] for i in range(leaves)], 1)
     coeff_t = fold(dot_bf16(own, w3[: 2 * RANK], NT)) * (1.0 / LN2)
-    l_ntr.wait()
-    up_t = dot_f32(coeff_t, ntr[0])
-    packed = jnp.concatenate([up_t[16 * k : 16 * (k + 1)] for k in range(4)], 1)
-    for p in range(n_sub):
-        ps[p] = packed[p * rows : (p + 1) * rows]
-
-    met = n_sub - 1 + n_y - 1 + z + has_lower.astype(jnp.int32) + has_upper.astype(jnp.int32)
-    pl.semaphore_wait(barrier, met)
-    for d in ss:
-        remote(ps.at[(s + d) % n_sub], ru.at[d], 8, sub_peer(d)).start()
-    for other in range(n_z - 1):
-        pl.when(other < z)(lambda other=other: signal(later, (other * n_y + y, s)))
+    coeff = coeff_t.T
+    column[0] = jnp.concatenate([coeff[: RANK // 2], coeff[RANK // 2 :]], 1)
+    pl.when(jnp.logical_not(starts_late))(enter)
+    along_z(column, 5, False)
 
     rim = RIM * LEAF
     first, last = pl.ds(0, rim), pl.ds(leaves * LEAF - rim, rim)
-    down = [remote(crd.at[:, first], hc.at[1], 0, lower), remote(vec.at[:, first], hv.at[1], 2, lower)]
-    up = [remote(crd.at[:, last], hc.at[0], 1, upper), remote(vec.at[:, last], hv.at[0], 3, upper)]
+    top, bottom = pl.ds(0, NV // 2), pl.ds(NV // 2, NV // 2)
+    down = [
+        remote(crd.at[:, first], hc.at[1], 0, lower),
+        remote(vec.at[top, first], hv.at[1, top], 2, lower),
+        remote(vec.at[bottom, first], hv.at[1, bottom], 9, lower),
+    ]
+    up = [
+        remote(crd.at[:, last], hc.at[0], 1, upper),
+        remote(vec.at[top, last], hv.at[0, top], 3, upper),
+        remote(vec.at[bottom, last], hv.at[0, bottom], 10, upper),
+    ]
 
     def start_all(copies):
         for copy in copies:
             copy.start()
 
-    def send_halo():
-        pl.when(has_lower)(lambda: start_all(down))
-        pl.when(has_upper)(lambda: start_all(up))
-
-    coeff = coeff_t.T
-    coeff = jnp.concatenate([coeff[:16], coeff[16:]], 1)
-    for k in range(3):
-        gy[0, 0, k] = coeff[4 * k : 4 * (k + 1)]
-    gz[0, 0] = coeff[12:16]
-    for d in ys:
-        remote(gy.at[0, 0], gy.at[0, d], 4, y_peer(d)).start()
+    lower_early = has_lower & jnp.logical_not(starts_late & (y == 0))
+    upper_early = has_upper & jnp.logical_not(starts_late & (y == n_y - 1))
+    lower_late = has_lower & starts_late & (y == 0)
+    upper_late = has_upper & starts_late & (y == n_y - 1)
 
     l_crd.wait()
-    send_halo()
+    pl.when(lower_early)(lambda: start_all(down))
+    pl.when(upper_early)(lambda: start_all(up))
     wide = 8 * LEAF
 
     def own_features(i, c):
@@ -209,43 +235,82 @@
         return c
 
     lax.fori_loop(0, leaves // 8, own_features, 0)
-    l_sk1.wait()
-    gs[0, 0, rows : rows + 1] = jnp.concatenate([sk1[0, 0:1], sk1[0, 1:2], jnp.zeros((1, 2 * RANK), F32)], 1)
-
-    remote(ru.at[ns1], ru.at[ns1], 8, sub_peer(1)).wait_recv()
-    total = ps[s]
-    for d in ss:
-        total = total + ru[d]
-    gs[0, 0, 0:rows] = total
-
     @pl.when(z < n_z - 1)
     def _():
         pl.semaphore_wait(later, n_z - 1 - z)
 
-    for d in zs:
-        remote(gs.at[0, 0], gs.at[0, d], 11, z_peer(d)).start()
-    for d in zs:
-        remote(gz.at[0, 0], gz.at[0, d], 5, z_peer(d)).start()
-
-    def pass_on():
-        remote(gs.at[0, nz1], gs.at[0, nz1], 11, z_peer(1)).wait_recv()
-        for d in ys:
-            remote(gs.at[0], gs.at[d], 7, y_peer(d)).start()
-        remote(gy.at[0, ny1], gy.at[0, ny1], 4, y_peer(1)).wait_recv()
-        for d in zs:
-            remote(gy.at[0], gy.at[d], 6, z_peer(d)).start()
-
-    passes_first = b >= n_branch // 2 - 1
-    pl.when(passes_first)(pass_on)
+    along_z(early, 8, True)
+    along_z(column, 5, True)
+    pl.when(lower_late)(lambda: start_all(down[:2]))
+    pl.when(upper_late)(lambda: start_all(up[:2]))
     l_sk2.wait()
     sk2t[...] = jnp.concatenate([sk2[0].T, sk2[1].T], 1)
+
+    def prepare_parts():
+        remote(info.at[ny1], info.at[ny1], 4, y_peer(1)).wait_recv()
+        remote(early.at[nz1], early.at[nz1], 8, z_peer(1)).wait_recv()
+        pl.when(lower_late)(lambda: start_all(down[2:]))
+        pl.when(upper_late)(lambda: start_all(up[2:]))
+        target = jnp.concatenate([info[(n_y - d) % n_y] for d in range(n_y)], 0)
+        group = [sk2t[pl.ds(z * n_y + (y + d) % n_y, 1)] for d in range(n_y)]
+        line = [jnp.concatenate([target[d : d + 1, RANK * k : RANK * (k + 1)] for d in range(n_y)], 1) for k in range(2)]
+        line += [jnp.concatenate([g[:, RANK * k : RANK * (k + 1)] for g in group], 1) for k in range(2)]
+        at = (jnp.concatenate(line + [jnp.zeros((4, n_y * RANK), F32)], 0) * SCALE).T
+        node_rows = [early[d, 8:9] for d in range(n_z)]
+        group_rows = [sk2t[pl.ds((z + n_z - d) % n_z * n_y + y, 1)] for d in range(n_z)]
+        for level, (source, scale) in enumerate(((node_rows, n_sub), (group_rows, 1))):
+            sx = jnp.concatenate([r[:, :RANK] for r in source], 1) * SCALE
+            sy = jnp.concatenate([r[:, RANK : 2 * RANK] for r in source], 1) * SCALE
+            dx = at[:, 2 * level : 2 * level + 1] - sx
+            dy = at[:, 2 * level + 1 : 2 * level + 2] - sy
+            names = []
+            for d in range(n_z):
+                name = ((z + n_z - d) % n_z * n_y + y) * scale + (s if scale > 1 else 0)
+                names.append(jnp.full((1, RANK), name.astype(F32), F32))
+            names = jnp.concatenate(names, 1)
+            count = jnp.zeros((n_y, n_z * RANK), F32)
+            for k in range(8):
+                lane = 2 * RANK + 8 * level + k
+                count = count + (target[:, lane : lane + 1] == names).astype(F32)
+            count = jnp.concatenate([jnp.broadcast_to(count[d : d + 1], (RANK, n_z * RANK)) for d in range(n_y)], 0)
+            tile = matern_of(dx * dx + dy * dy) * (count * LN2)
+            if level == 1:
+                moved = []
+                for d in range(n_z):
+                    transfer = jnp.concatenate([early[d, 0:8, RANK * k : RANK * (k + 1)] for k in range(4)], 0)
+                    moved.append(dot_high(tile[:, d * RANK : (d + 1) * RANK], transfer, NT))
+                tile = jnp.concatenate(moved, 1)
+            high, low = split(tile)
+            mix[level * n_y * RANK : (level + 1) * n_y * RANK] = jnp.concatenate([high, high, low], 1)
+
+    def send_parts():
+        remote(column.at[nz1], column.at[nz1], 5, z_peer(1)).wait_recv()
+        coeffs = []
+        for d in range(n_z):
+            coeffs += [column[d, :, :NV], column[d, :, NV:]]
+        high, low = split(jnp.concatenate(coeffs, 0))
+        fields = dot_bf16(mix[...], jnp.concatenate([high, low, high], 0))
+        for d in range(n_y):
+            at = d * RANK
+            part[d] = jnp.concatenate([fields[at : at + RANK], fields[n_y * RANK + at : n_y * RANK + at + RANK]], 1)
+        for d in ys:
+            remote(part.at[d], parts.at[d], 6, y_peer(d)).start()
+
+    def both_parts():
+        prepare_parts()
+        send_parts()
+
+    parts_first = z >= n_z // 2 - 1
+    pl.when(parts_first)(both_parts)
     l_near.wait()
-    l_list1.wait()
-    l_list2.wait()
-
-    def rims(wait_k, take):
+
+    def arrived(copies):
+        for copy in copies:
+            copy.wait_recv()
+
+    def rims(waits, take):
         for side, there, copies in ((0, has_lower, up), (1, has_upper, down)):
-            pl.when(there)(lambda copies=copies: copies[wait_k].wait_recv())
+            pl.when(there)(lambda copies=copies: arrived(copies[waits]))
             take(side, side * (RIM + leaves))
 
     def rim_features(side, base):
@@ -260,8 +325,8 @@
             vw[base + i, :NV] = high
             vw[base + i, NV:] = low
 
-    rims(0, rim_features)
-    rims(1, rim_vectors)
+    rims(slice(0, 1), rim_features)
+    rims(slice(1, 3), rim_vectors)
 
     def near_leaves(first_leaf):
         items = [(first_leaf + u, pair) for u in range(BLOCK) for pair in PAIRS]
@@ -293,60 +358,33 @@
                     out[:, leaf_cols(i)] = fold(acc) + NUGGET * vec[:, leaf_cols(i)]
                     acc = None
 
-    def place_of(branch):
-        return (z + n_z - branch // n_y) % n_z, (y + n_y - branch % n_y) % n_y
-
-    def far_tile(target, sources):
-        column = (jnp.concatenate([target[:, :RANK], target[:, RANK : 2 * RANK]], 0) * SCALE).T
-        sx = jnp.concatenate([row[:, :RANK] for row in sources], 1) * SCALE
-        sy = jnp.concatenate([row[:, RANK : 2 * RANK] for row in sources], 1) * SCALE
-        dx = sx - column[:, 0:1]
-        dy = sy - column[:, 1:2]
-        return matern_of(dx * dx + dy * dy) * LN2
-
-    def group_field():
-        remote(gs.at[ny1], gs.at[ny1], 7, y_peer(1)).wait_recv()
-        remote(gz.at[0, nz1], gz.at[0, nz1], 5, z_peer(1)).wait_recv()
+    def send_group():
+        remote(parts.at[ny1], parts.at[ny1], 6, y_peer(1)).wait_recv()
+        field = part[0]
         for d in ys:
-            remote(gz.at[0], gz.at[d], 9, y_peer(d)).start()
-        sources, coeffs = [], []
-        for k in range(8):
-            m = list2[0, k]
-            dz, dy = place_of(m)
-            sources.append(sk2t[pl.ds(m, 1)])
-            block = gs[dy, dz][0:rows]
-            coeffs.append(jnp.concatenate([block[:, RANK * q : RANK * (q + 1)] for q in range(4)], 0))
-        field = dot_f32(jnp.concatenate(coeffs, 1), far_tile(sk2t[pl.ds(b, 1)], sources), NT)
-        fc[0] = jnp.concatenate([field[rows * q : rows * (q + 1)] for q in range(4)], 1)
+            field = field + parts[d]
+        own_field[...] = field
+        fc[0] = jnp.concatenate([field[: RANK // 2, NV:], field[RANK // 2 :, NV:]], 1)
         for d in ss:
-            remote(fc.at[0], fc.at[d], 10, sub_peer(d)).start()
-
-    blocks = leaves // BLOCK
-    pass_step = jnp.where(passes_first, blocks, jnp.where(z >= n_z // 4, 1, 2))
-    group_step = jnp.where(z >= n_z // 2, 2, jnp.where(z >= n_z // 4, 3, blocks))
+            remote(fc.at[0], fc.at[d], 7, sub_peer(d)).start()
+
+    parts_step = jnp.where(parts_first, leaves // BLOCK, 1)
+    group_step = jnp.where(parts_first, 2, 3)
 
     def near_block(t, c):
-        pl.when(t == pass_step)(pass_on)
-        pl.when(t == group_step)(group_field)
+        pl.when(t == parts_step)(both_parts)
+        pl.when(t == group_step)(send_group)
         near_leaves(t * BLOCK)
         return c
 
-    lax.fori_loop(0, blocks, near_block, 0)
-    pl.when(group_step == blocks)(group_field)
-
-    remote(gy.at[nz1], gy.at[nz1], 6, z_peer(1)).wait_recv()
-    remote(gz.at[ny1], gz.at[ny1], 9, y_peer(1)).wait_recv()
-    sources, coeffs = [], []
-    for k in range(8):
-        dz, dy = place_of(list1[0, k] // n_sub)
-        sources.append(gs[dy, dz][rows : rows + 1])
-        block = jnp.concatenate([gy[dz, dy, 0], gy[dz, dy, 1], gy[dz, dy, 2], gz[dy, dz]], 0)
-        coeffs += [block[:, :NV], block[:, NV:]]
-    field = dot_f32(far_tile(gs[0, 0][rows : rows + 1], sources), jnp.concatenate(coeffs, 0))
-    remote(fc.at[ns1], fc.at[ns1], 10, sub_peer(1)).wait_recv()
-    packed = jnp.concatenate([fc[(s + n_sub - p) % n_sub] for p in range(n_sub)], 0)
-    group_t = jnp.concatenate([packed[:, RANK * q : RANK * (q + 1)] for q in range(4)], 0)
-    field = field + dot_f32(ntr[0], group_t, NT)
+    lax.fori_loop(0, leaves // BLOCK, near_block, 0)
+
+    remote(fc.at[ns1], fc.at[ns1], 7, sub_peer(1)).wait_recv()
+    group = fc[0]
+    for d in ss:
+        group = group + fc[d]
+    group = jnp.concatenate([group[:, :NV], group[:, NV:]], 0)
+    field = own_field[:, :NV] + dot_f32(ntr[0], group)
     fh, fl = split(field.T)
     lhs = jnp.concatenate([fh, fh, fl], 1)
 
@@ -363,10 +401,7 @@
 
     pl.when(has_lower)(lambda: finish(down))
     pl.when(has_upper)(lambda: finish(up))
-    for ref, k in (
-        (gy.at[0, ny1], 4), (gz.at[0, nz1], 5), (gy.at[nz1], 6), (gs.at[ny1], 7),
-        (ru.at[ns1], 8), (gz.at[ny1], 9), (fc.at[ns1], 10), (gs.at[0, nz1], 11),
-    ):
+    for ref, k in ((info.at[ny1], 4), (column.at[nz1], 5), (parts.at[ny1], 6), (fc.at[ns1], 7), (early.at[nz1], 8)):
         remote(ref, ref, k, sub_peer(1)).wait_send()
 
 
@@ -375,13 +410,13 @@
     n_z = n_branch // n_y
     leaves = leaf_transfer.shape[0]
     window = leaves + 2 * RIM
-    rows = 16 // n_sub
     rim = RIM * LEAF
     operands = (
         vectors, coords, basis, leaf_transfer, node_transfer, skel_one,
         jnp.transpose(skel_two, (1, 2, 0)), near_list.T, list_one, list_two,
     )
-    held = [pltpu.VMEM(a.shape, F32) for a in operands[:7]] + [pltpu.SMEM(a.shape, jnp.int32) for a in operands[7:]]
+    held = [pltpu.VMEM(a.shape, F32) for a in operands[:7]] + [pltpu.SMEM(operands[7].shape, jnp.int32)]
+    held += [pltpu.VMEM(a.shape, jnp.int32) for a in operands[8:]]
     return pl.pallas_call(
         functools.partial(kernel, sizes),
         out_shape=jax.ShapeDtypeStruct(vectors.shape, F32),
@@ -396,15 +431,17 @@
             pltpu.VMEM((FEATURES, leaves * LEAF), BF16),
             pltpu.VMEM((3 * RANK, leaves * LEAF), BF16),
             pltpu.VMEM((n_branch, 2 * RANK), F32),
-            pltpu.VMEM((n_z, n_y, 3, 4, 128), F32),
-            pltpu.VMEM((n_y, n_z, 4, 128), F32),
-            pltpu.VMEM((n_y, n_z, 2 * rows, 128), F32),
-            pltpu.VMEM((n_sub, rows, 128), F32),
-            pltpu.VMEM((n_sub, rows, 128), F32),
-            pltpu.VMEM((n_sub, rows, 128), F32),
+            pltpu.VMEM((n_y, 1, 128), F32),
+            pltpu.VMEM((n_z, 9, 128), F32),
+            pltpu.VMEM((n_z, RANK // 2, 128), F32),
+            pltpu.VMEM((2 * n_y * RANK, 3 * n_z * RANK), BF16),
+            pltpu.VMEM((n_y, RANK, 128), F32),
+            pltpu.VMEM((n_y, RANK, 128), F32),
+            pltpu.VMEM((RANK, 128), F32),
+            pltpu.VMEM((n_sub, RANK // 2, 128), F32),
             pltpu.SemaphoreType.DMA((10,)),
-            pltpu.SemaphoreType.DMA((12,)),
-            pltpu.SemaphoreType.DMA((12,)),
+            pltpu.SemaphoreType.DMA((11,)),
+            pltpu.SemaphoreType.DMA((11,)),
             pltpu.SemaphoreType.REGULAR,
         ],
         compiler_params=pltpu.CompilerParams(

time: 40.3 us -> 37.4 us (0.928); the launches traced: 39.6 us -> 37.3 us
  Pallas kernels: 37.3 us -> 35 us
    pallas_call x1, Pallas kernels: 37.3 us -> 35 us  [body(): pl.pallas_call(functools.partial(kernel, sizes), out_shape=jax.ShapeDtype...]
where the time goes in v3:
time: 37.4 us; the launch traced here: 37.3 us
  Pallas kernels  35 us (94%)
  local copies, waits for them, and re-layouts  2.27 us (6%)
    pallas_call x1, Pallas kernels, body(): pl.pallas_call(functools.partial(kernel, sizes), out_shape=jax.ShapeDtype...  35 us
    unnamed x1, local copies, waits for them, and re-layouts  2.27 us

profile of v3, /device:TPU:1, one launch (start us, length us, event | category | flops | bytes accessed | tf_op | source)
XLA Modules:
  0.0 37.3 jit_solution(5951400777971090774)
XLA Ops:
  0.0 35.0 %h2_product.1 = f32[64,4096]{1,0:T(8,128)} custom-call(f32[64,4096]{1,0:T(8,128)} %refs_0_.1, f32[2,4096]{1,0:T(2,128)} %refs_1_.1, f32[32,4096]{1,0:T(8,128)} %refs_2_.1, f32[32,32,32]{2,1,0:T(8,128)} %refs_3_.1, f32[1,32,32]{2,1,0:T(8,128)} %refs_4_.1, f32[1,2,32]{2,1,0:T(2,128)} %refs_5_.1, f32[2,32,64]{2,1,0:T(8,128)} %bitcast.2, s32[9,32]{1,0:T(8,128)} %bitcast.3, ...), custom_call_target="tpu_custom_call" | custom-call | tf_op jit(solution)/shard_map/h2_product/pallas_call | solution.py:420
  35.0 2.3 %copy.12 = f32[64,4096]{1,0:T(8,128)} copy(f32[64,4096]{1,0:T(8,128)} %h2_product.1) | data formatting | bytes 2097152

commit v4 on v3

--- a/solution.py
+++ b/solution.py
@@ -26,6 +26,7 @@
 CENTRE = 1.5
 VMEM_LIMIT = 62 * 2**20
 FEATURES = 32
+CHUNKS = 4
 NN, NT, TN = ((1,), (0,)), ((1,), (1,)), ((0,), (0,))
 
 
@@ -82,9 +83,9 @@
 
 
 def kernel(sizes, *refs):
-    operands, out = refs[:10], refs[10]
+    operands, result = refs[:10], refs[10]
     vec, crd, bas, ltr, ntr, sk1, sk2, near, list1, list2 = refs[11:21]
-    hv, hc, vw, fs, ft, w3, sk2t, info, early, column, mix, part, parts, own_field, fc, load, send, recv, later = refs[21:]
+    out, hv, hc, vw, fs, ft, w3, sk2t, info, early, column, mix, part, parts, own_field, fc, load, store, send, recv, later = refs[21:]
     n_branch, n_sub, n_y = sizes
     n_z = n_branch // n_y
     leaves = ltr.shape[0]
@@ -116,7 +117,7 @@
     def signal(sem, peer):
         pl.semaphore_signal(sem, inc=1, device_id=peer, device_id_type=MESH)
 
-    ys, zs, ss = range(1, n_y), range(1, n_z), range(1, n_sub)
+    ys, zs, ss = (sorted(range(1, n), key=lambda d: (-min(d, n - d), d)) for n in (n_y, n_z, n_sub))
     has_lower, has_upper = b > 0, b < n_branch - 1
     lower, upper = (b - 1, s), (b + 1, s)
 
@@ -156,8 +157,6 @@
             remote(info.at[0], info.at[d], 4, y_peer(d)).start()
         along_z(early, 8, False)
 
-    pl.when(starts_late)(enter)
-
     for side, missing in ((0, b == 0), (1, b == n_branch - 1)):
 
         @pl.when(missing)
@@ -190,6 +189,7 @@
         return c
 
     lax.fori_loop(0, leaves, own_vectors, 0, unroll=8)
+    pl.when(starts_late)(enter)
     own = jnp.concatenate([vw[RIM + i] for i in range(leaves)], 1)
     coeff_t = fold(dot_bf16(own, w3[: 2 * RANK], NT)) * (1.0 / LN2)
     coeff = coeff_t.T
@@ -242,14 +242,14 @@
     along_z(early, 8, True)
     along_z(column, 5, True)
     pl.when(lower_late)(lambda: start_all(down[:2]))
-    pl.when(upper_late)(lambda: start_all(up[:2]))
     l_sk2.wait()
     sk2t[...] = jnp.concatenate([sk2[0].T, sk2[1].T], 1)
 
     def prepare_parts():
         remote(info.at[ny1], info.at[ny1], 4, y_peer(1)).wait_recv()
+        pl.when(lower_late)(lambda: start_all(down[2:]))
+        pl.when(upper_late)(lambda: start_all(up[:2]))
         remote(early.at[nz1], early.at[nz1], 8, z_peer(1)).wait_recv()
-        pl.when(lower_late)(lambda: start_all(down[2:]))
         pl.when(upper_late)(lambda: start_all(up[2:]))
         target = jnp.concatenate([info[(n_y - d) % n_y] for d in range(n_y)], 0)
         group = [sk2t[pl.ds(z * n_y + (y + d) % n_y, 1)] for d in range(n_y)]
@@ -388,12 +388,15 @@
     fh, fl = split(field.T)
     lhs = jnp.concatenate([fh, fh, fl], 1)
 
-    def far(i, c):
-        cols = pl.ds(pl.multiple_of(i * 2 * LEAF, 2 * LEAF), 2 * LEAF)
-        out[:, cols] += dot_bf16(lhs, w3[:, cols])
-        return c
-
-    lax.fori_loop(0, leaves // 2, far, 0, unroll=8)
+    wide = leaves * LEAF // CHUNKS
+    stores = []
+    for chunk in range(CHUNKS):
+        for i in range(wide // (2 * LEAF)):
+            cols = pl.ds(chunk * wide + i * 2 * LEAF, 2 * LEAF)
+            out[:, cols] += dot_bf16(lhs, w3[:, cols])
+        cols = pl.ds(chunk * wide, wide)
+        stores.append(pltpu.make_async_copy(out.at[:, cols], result.at[:, cols], store.at[chunk]))
+        stores[-1].start()
 
     def finish(copies):
         for copy in copies:
@@ -403,6 +406,8 @@
     pl.when(has_upper)(lambda: finish(up))
     for ref, k in ((info.at[ny1], 4), (column.at[nz1], 5), (parts.at[ny1], 6), (fc.at[ns1], 7), (early.at[nz1], 8)):
         remote(ref, ref, k, sub_peer(1)).wait_send()
+    for copy in stores:
+        copy.wait()
 
 
 def body(sizes, vectors, coords, basis, leaf_transfer, node_transfer, skel_one, skel_two, near_list, list_one, list_two):
@@ -421,9 +426,10 @@
         functools.partial(kernel, sizes),
         out_shape=jax.ShapeDtypeStruct(vectors.shape, F32),
         in_specs=[pl.BlockSpec(memory_space=pltpu.HBM)] * 10,
-        out_specs=pl.BlockSpec(memory_space=pltpu.VMEM),
+        out_specs=pl.BlockSpec(memory_space=pltpu.HBM),
         scratch_shapes=[
             *held,
+            pltpu.VMEM(vectors.shape, F32),
             pltpu.VMEM((2, NV, rim), F32),
             pltpu.VMEM((2, 2, rim), F32),
             pltpu.VMEM((window, 2 * NV, LEAF), BF16),
@@ -440,6 +446,7 @@
             pltpu.VMEM((RANK, 128), F32),
             pltpu.VMEM((n_sub, RANK // 2, 128), F32),
             pltpu.SemaphoreType.DMA((10,)),
+            pltpu.SemaphoreType.DMA((CHUNKS,)),
             pltpu.SemaphoreType.DMA((11,)),
             pltpu.SemaphoreType.DMA((11,)),
             pltpu.SemaphoreType.REGULAR,

time: 37.4 us -> 35.1 us (0.939)
  Pallas kernels: 35 us -> 32.6 us
    pallas_call x1, Pallas kernels: 35 us -> 32.6 us  [body(): pl.pallas_call(functools.partial(kernel, sizes), out_shape=jax.ShapeDtype...]
where the time goes in v4:
time: 35.1 us; the launch traced here: 34.9 us
  Pallas kernels  32.6 us (93%)
  local copies, waits for them, and re-layouts  2.27 us (6%)
    pallas_call x1, Pallas kernels, body(): pl.pallas_call(functools.partial(kernel, sizes), out_shape=jax.ShapeDtype...  32.6 us
    unnamed x1, local copies, waits for them, and re-layouts  2.27 us

profile of v4, /device:TPU:1, one launch (start us, length us, event | category | flops | bytes accessed | tf_op | source)
XLA Modules:
  0.0 34.9 jit_solution(1332090203163426989)
XLA Ops:
  0.0 32.6 %h2_product.1 = f32[64,4096]{1,0:T(8,128)} custom-call(f32[64,4096]{1,0:T(8,128)} %refs_0_.1, f32[2,4096]{1,0:T(2,128)} %refs_1_.1, f32[32,4096]{1,0:T(8,128)} %refs_2_.1, f32[32,32,32]{2,1,0:T(8,128)} %refs_3_.1, f32[1,32,32]{2,1,0:T(8,128)} %refs_4_.1, f32[1,2,32]{2,1,0:T(2,128)} %refs_5_.1, f32[2,32,64]{2,1,0:T(8,128)} %bitcast.2, s32[9,32]{1,0:T(8,128)} %bitcast.3, ...), custom_call_target="tpu_custom_call" | custom-call | tf_op jit(solution)/shard_map/h2_product/pallas_call | solution.py:425
  32.6 2.3 %copy.12 = f32[64,4096]{1,0:T(8,128)} copy(f32[64,4096]{1,0:T(8,128)} %h2_product.1) | data formatting | bytes 2097152

commit v5 on v3

--- a/solution.py
+++ b/solution.py
@@ -24,7 +24,7 @@
 PAIRS = ((0, 1), (2, 3), (4, 5), (6, 7), (8,))
 EXACT = lax.Precision.HIGHEST
 CENTRE = 1.5
-VMEM_LIMIT = 62 * 2**20
+VMEM_LIMIT = 48 * 2**20
 FEATURES = 32
 NN, NT, TN = ((1,), (0,)), ((1,), (1,)), ((0,), (0,))
 
@@ -84,7 +84,7 @@
 def kernel(sizes, *refs):
     operands, out = refs[:10], refs[10]
     vec, crd, bas, ltr, ntr, sk1, sk2, near, list1, list2 = refs[11:21]
-    hv, hc, vw, fs, ft, w3, sk2t, info, early, column, mix, part, parts, own_field, fc, load, send, recv, later = refs[21:]
+    hv, hc, vw, fs, ft, w3, sk2t, info, early, column, places, group_tile, mix, part, parts, own_field, fc, load, send, recv, later = refs[21:]
     n_branch, n_sub, n_y = sizes
     n_z = n_branch // n_y
     leaves = ltr.shape[0]
@@ -116,7 +116,7 @@
     def signal(sem, peer):
         pl.semaphore_signal(sem, inc=1, device_id=peer, device_id_type=MESH)
 
-    ys, zs, ss = range(1, n_y), range(1, n_z), range(1, n_sub)
+    ys, zs, ss = (sorted(range(1, n), key=lambda d: (-min(d, n - d), d)) for n in (n_y, n_z, n_sub))
     has_lower, has_upper = b > 0, b < n_branch - 1
     lower, upper = (b - 1, s), (b + 1, s)
 
@@ -156,8 +156,6 @@
             remote(info.at[0], info.at[d], 4, y_peer(d)).start()
         along_z(early, 8, False)
 
-    pl.when(starts_late)(enter)
-
     for side, missing in ((0, b == 0), (1, b == n_branch - 1)):
 
         @pl.when(missing)
@@ -190,6 +188,7 @@
         return c
 
     lax.fori_loop(0, leaves, own_vectors, 0, unroll=8)
+    pl.when(starts_late)(enter)
     own = jnp.concatenate([vw[RIM + i] for i in range(leaves)], 1)
     coeff_t = fold(dot_bf16(own, w3[: 2 * RANK], NT)) * (1.0 / LN2)
     coeff = coeff_t.T
@@ -235,53 +234,69 @@
         return c
 
     lax.fori_loop(0, leaves // 8, own_features, 0)
-    @pl.when(z < n_z - 1)
-    def _():
-        pl.semaphore_wait(later, n_z - 1 - z)
-
-    along_z(early, 8, True)
-    along_z(column, 5, True)
-    pl.when(lower_late)(lambda: start_all(down[:2]))
-    pl.when(upper_late)(lambda: start_all(up[:2]))
     l_sk2.wait()
     sk2t[...] = jnp.concatenate([sk2[0].T, sk2[1].T], 1)
 
-    def prepare_parts():
+    def source_names(scale, offset):
+        names = []
+        for d in range(n_z):
+            name = ((z + n_z - d) % n_z * n_y + y) * scale + offset
+            names.append(jnp.full((1, RANK), name.astype(F32), F32))
+        return jnp.concatenate(names, 1)
+
+    def counted_tile(at, target, source, names, lane):
+        sx = jnp.concatenate([r[:, :RANK] for r in source], 1) * SCALE
+        sy = jnp.concatenate([r[:, RANK : 2 * RANK] for r in source], 1) * SCALE
+        dx = at[:, 0:1] - sx
+        dy = at[:, 1:2] - sy
+        count = jnp.zeros((n_y, n_z * RANK), F32)
+        for k in range(8):
+            count = count + (target[:, lane + k : lane + k + 1] == names).astype(F32)
+        count = jnp.concatenate([jnp.broadcast_to(count[d : d + 1], (RANK, n_z * RANK)) for d in range(n_y)], 0)
+        return matern_of(dx * dx + dy * dy) * (count * LN2)
+
+    def targets():
+        return jnp.concatenate([info[(n_y - d) % n_y] for d in range(n_y)], 0)
+
+    def keep_mix(level, tile):
+        high, low = split(tile)
+        mix[level * n_y * RANK : (level + 1) * n_y * RANK] = jnp.concatenate([high, high, low], 1)
+
+    def prepare_groups():
         remote(info.at[ny1], info.at[ny1], 4, y_peer(1)).wait_recv()
-        remote(early.at[nz1], early.at[nz1], 8, z_peer(1)).wait_recv()
-        pl.when(lower_late)(lambda: start_all(down[2:]))
-        pl.when(upper_late)(lambda: start_all(up[2:]))
-        target = jnp.concatenate([info[(n_y - d) % n_y] for d in range(n_y)], 0)
+        target = targets()
         group = [sk2t[pl.ds(z * n_y + (y + d) % n_y, 1)] for d in range(n_y)]
         line = [jnp.concatenate([target[d : d + 1, RANK * k : RANK * (k + 1)] for d in range(n_y)], 1) for k in range(2)]
         line += [jnp.concatenate([g[:, RANK * k : RANK * (k + 1)] for g in group], 1) for k in range(2)]
         at = (jnp.concatenate(line + [jnp.zeros((4, n_y * RANK), F32)], 0) * SCALE).T
+        places[...] = at
+        group_rows = [sk2t[pl.ds((z + n_z - d) % n_z * n_y + y, 1)] for d in range(n_z)]
+        group_tile[...] = counted_tile(at[:, 2:4], target, group_rows, source_names(1, 0), 2 * RANK + 8)
+
+    pl.when(z < n_z // 2)(prepare_groups)
+
+    @pl.when(z < n_z - 1)
+    def _():
+        pl.semaphore_wait(later, n_z - 1 - z)
+
+    along_z(early, 8, True)
+    along_z(column, 5, True)
+    pl.when(lower_late)(lambda: start_all(down[:2]))
+    @pl.when(starts_late)
+    def _():
+        prepare_groups()
+        pl.when(lower_late)(lambda: start_all(down[2:]))
+        pl.when(upper_late)(lambda: start_all(up))
+
+    def prepare_nodes():
+        remote(early.at[nz1], early.at[nz1], 8, z_peer(1)).wait_recv()
+        moved = []
+        for d in range(n_z):
+            transfer = jnp.concatenate([early[d, 0:8, RANK * k : RANK * (k + 1)] for k in range(4)], 0)
+            moved.append(dot_high(group_tile[:, d * RANK : (d + 1) * RANK], transfer, NT))
+        keep_mix(1, jnp.concatenate(moved, 1))
         node_rows = [early[d, 8:9] for d in range(n_z)]
-        group_rows = [sk2t[pl.ds((z + n_z - d) % n_z * n_y + y, 1)] for d in range(n_z)]
-        for level, (source, scale) in enumerate(((node_rows, n_sub), (group_rows, 1))):
-            sx = jnp.concatenate([r[:, :RANK] for r in source], 1) * SCALE
-            sy = jnp.concatenate([r[:, RANK : 2 * RANK] for r in source], 1) * SCALE
-            dx = at[:, 2 * level : 2 * level + 1] - sx
-            dy = at[:, 2 * level + 1 : 2 * level + 2] - sy
-            names = []
-            for d in range(n_z):
-                name = ((z + n_z - d) % n_z * n_y + y) * scale + (s if scale > 1 else 0)
-                names.append(jnp.full((1, RANK), name.astype(F32), F32))
-            names = jnp.concatenate(names, 1)
-            count = jnp.zeros((n_y, n_z * RANK), F32)
-            for k in range(8):
-                lane = 2 * RANK + 8 * level + k
-                count = count + (target[:, lane : lane + 1] == names).astype(F32)
-            count = jnp.concatenate([jnp.broadcast_to(count[d : d + 1], (RANK, n_z * RANK)) for d in range(n_y)], 0)
-            tile = matern_of(dx * dx + dy * dy) * (count * LN2)
-            if level == 1:
-                moved = []
-                for d in range(n_z):
-                    transfer = jnp.concatenate([early[d, 0:8, RANK * k : RANK * (k + 1)] for k in range(4)], 0)
-                    moved.append(dot_high(tile[:, d * RANK : (d + 1) * RANK], transfer, NT))
-                tile = jnp.concatenate(moved, 1)
-            high, low = split(tile)
-            mix[level * n_y * RANK : (level + 1) * n_y * RANK] = jnp.concatenate([high, high, low], 1)
+        keep_mix(0, counted_tile(places[:, 0:2], targets(), node_rows, source_names(n_sub, s), 2 * RANK))
 
     def send_parts():
         remote(column.at[nz1], column.at[nz1], 5, z_peer(1)).wait_recv()
@@ -297,10 +312,11 @@
             remote(part.at[d], parts.at[d], 6, y_peer(d)).start()
 
     def both_parts():
-        prepare_parts()
+        prepare_nodes()
         send_parts()
 
-    parts_first = z >= n_z // 2 - 1
+    in_second_half = z >= n_z // 2 - 1
+    parts_first = in_second_half | (y == n_y - 1)
     pl.when(parts_first)(both_parts)
     l_near.wait()
 
@@ -369,7 +385,7 @@
             remote(fc.at[0], fc.at[d], 7, sub_peer(d)).start()
 
     parts_step = jnp.where(parts_first, leaves // BLOCK, 1)
-    group_step = jnp.where(parts_first, 2, 3)
+    group_step = jnp.where(in_second_half, 2, 3)
 
     def near_block(t, c):
         pl.when(t == parts_step)(both_parts)
@@ -384,16 +400,13 @@
     for d in ss:
         group = group + fc[d]
     group = jnp.concatenate([group[:, :NV], group[:, NV:]], 0)
-    field = own_field[:, :NV] + dot_f32(ntr[0], group)
+    field = own_field[:, :NV] + dot_high(ntr[0], group)
     fh, fl = split(field.T)
     lhs = jnp.concatenate([fh, fh, fl], 1)
 
-    def far(i, c):
-        cols = pl.ds(pl.multiple_of(i * 2 * LEAF, 2 * LEAF), 2 * LEAF)
+    for i in range(leaves // 2):
+        cols = pl.ds(i * 2 * LEAF, 2 * LEAF)
         out[:, cols] += dot_bf16(lhs, w3[:, cols])
-        return c
-
-    lax.fori_loop(0, leaves // 2, far, 0, unroll=8)
 
     def finish(copies):
         for copy in copies:
@@ -419,7 +432,7 @@
     held += [pltpu.VMEM(a.shape, jnp.int32) for a in operands[8:]]
     return pl.pallas_call(
         functools.partial(kernel, sizes),
-        out_shape=jax.ShapeDtypeStruct(vectors.shape, F32),
+        out_shape=pltpu.VMEM(vectors.shape, F32),
         in_specs=[pl.BlockSpec(memory_space=pltpu.HBM)] * 10,
         out_specs=pl.BlockSpec(memory_space=pltpu.VMEM),
         scratch_shapes=[
@@ -434,6 +447,8 @@
             pltpu.VMEM((n_y, 1, 128), F32),
             pltpu.VMEM((n_z, 9, 128), F32),
             pltpu.VMEM((n_z, RANK // 2, 128), F32),
+            pltpu.VMEM((n_y * RANK, 8), F32),
+            pltpu.VMEM((n_y * RANK, n_z * RANK), F32),
             pltpu.VMEM((2 * n_y * RANK, 3 * n_z * RANK), BF16),
             pltpu.VMEM((n_y, RANK, 128), F32),
             pltpu.VMEM((n_y, RANK, 128), F32),
@@ -448,7 +463,7 @@
             collective_id=0, has_side_effects=True, vmem_limit_bytes=VMEM_LIMIT
         ),
         name="h2_product",
-    )(*operands)
+    )(*[pltpu.with_memory_space_constraint(a, pltpu.HBM) for a in operands])
 
 
 def solution(mesh, y_count=Y_COUNT):

time: 37.4 us -> 32.2 us (0.86)
  Pallas kernels: 35 us -> 31.1 us
  local copies, waits for them, and re-layouts: 2.27 us -> 0.97 us
    pallas_call x1, Pallas kernels: 35 us -> 31.1 us  [body(): pl.pallas_call(functools.partial(kernel, sizes), out_shape=pltpu.VMEM(vec...]
    unnamed x1, local copies, waits for them, and re-layouts: 2.27 us -> 0.97 us
where the time goes in v5:
time: 32.2 us; the launch traced here: 32.1 us
  Pallas kernels  31.1 us (97%)
  local copies, waits for them, and re-layouts  0.97 us (3%)
    pallas_call x1, Pallas kernels, body(): pl.pallas_call(functools.partial(kernel, sizes), out_shape=pltpu.VMEM(vec...  31.1 us
    unnamed x1, local copies, waits for them, and re-layouts  0.97 us

profile of v5, /device:TPU:1, one launch (start us, length us, event | category | flops | bytes accessed | tf_op | source)
XLA Modules:
  0.0 32.1 jit_solution(7975383102450051276)
XLA Ops:
  0.0 31.1 %h2_product.1 = f32[64,4096]{1,0:T(8,128)S(1)} custom-call(f32[64,4096]{1,0:T(8,128)} %refs_0_.1, f32[2,4096]{1,0:T(2,128)} %refs_1_.1, f32[32,4096]{1,0:T(8,128)} %refs_2_.1, f32[32,32,32]{2,1,0:T(8,128)} %refs_3_.1, f32[1,32,32]{2,1,0:T(8,128)} %refs_4_.1, f32[1,2,32]{2,1,0:T(2,128)} %refs_5_.1, f32[2,32,64]{2,1,0:T(8,128)} %bitcast.2, s32[9,32]{1,0:T(8,128)} %bitcast.3, ...), custom_call_target="tpu_custom_call" | custom-call | tf_op jit(solution)/shard_map/h2_product/pallas_call | solution.py:433
  31.1 1.0 %copy.12 = f32[64,4096]{1,0:T(8,128)} copy(f32[64,4096]{1,0:T(8,128)S(1)} %h2_product.1) | data formatting | bytes 2097152

commit v6 on v5

--- a/solution.py
+++ b/solution.py
@@ -84,7 +84,7 @@
 def kernel(sizes, *refs):
     operands, out = refs[:10], refs[10]
     vec, crd, bas, ltr, ntr, sk1, sk2, near, list1, list2 = refs[11:21]
-    hv, hc, vw, fs, ft, w3, sk2t, info, early, column, places, group_tile, mix, part, parts, own_field, fc, load, send, recv, later = refs[21:]
+    hv, hc, vw, fs, ft, w3, sk2t, info, early, column, places, group_tile, mix, group_part, group_parts, node_part, node_parts, fc, load, send, recv, later = refs[21:]
     n_branch, n_sub, n_y = sizes
     n_z = n_branch // n_y
     leaves = ltr.shape[0]
@@ -96,8 +96,8 @@
 
     loads = [pltpu.make_async_copy(operands[k], refs[11 + k], load.at[k]) for k in range(10)]
     l_vec, l_crd, l_bas, l_ltr, l_ntr, l_sk1, l_sk2, l_near, l_list1, l_list2 = loads
-    for copy in (l_ltr, l_bas, l_vec, l_crd, l_ntr, l_sk1, l_sk2, l_near, l_list1, l_list2):
-        copy.start()
+    l_ltr.start()
+    l_bas.start()
 
     def y_peer(d):
         return z * n_y + (y + d) % n_y, s
@@ -156,6 +156,9 @@
             remote(info.at[0], info.at[d], 4, y_peer(d)).start()
         along_z(early, 8, False)
 
+    for copy in (l_vec, l_ntr, l_sk1, l_list1, l_list2, l_crd, l_sk2, l_near):
+        copy.start()
+
     for side, missing in ((0, b == 0), (1, b == n_branch - 1)):
 
         @pl.when(missing)
@@ -188,12 +191,13 @@
         return c
 
     lax.fori_loop(0, leaves, own_vectors, 0, unroll=8)
-    pl.when(starts_late)(enter)
+    enters_first = starts_late & (y >= 2) & (y <= n_y - 2)
+    pl.when(enters_first)(enter)
     own = jnp.concatenate([vw[RIM + i] for i in range(leaves)], 1)
     coeff_t = fold(dot_bf16(own, w3[: 2 * RANK], NT)) * (1.0 / LN2)
     coeff = coeff_t.T
     column[0] = jnp.concatenate([coeff[: RANK // 2], coeff[RANK // 2 :]], 1)
-    pl.when(jnp.logical_not(starts_late))(enter)
+    pl.when(jnp.logical_not(enters_first))(enter)
     along_z(column, 5, False)
 
     rim = RIM * LEAF
@@ -214,13 +218,11 @@
         for copy in copies:
             copy.start()
 
-    lower_early = has_lower & jnp.logical_not(starts_late & (y == 0))
     upper_early = has_upper & jnp.logical_not(starts_late & (y == n_y - 1))
-    lower_late = has_lower & starts_late & (y == 0)
     upper_late = has_upper & starts_late & (y == n_y - 1)
 
     l_crd.wait()
-    pl.when(lower_early)(lambda: start_all(down))
+    pl.when(has_lower)(lambda: start_all(down))
     pl.when(upper_early)(lambda: start_all(up))
     wide = 8 * LEAF
 
@@ -275,17 +277,24 @@
 
     pl.when(z < n_z // 2)(prepare_groups)
 
-    @pl.when(z < n_z - 1)
-    def _():
-        pl.semaphore_wait(later, n_z - 1 - z)
-
-    along_z(early, 8, True)
-    along_z(column, 5, True)
-    pl.when(lower_late)(lambda: start_all(down[:2]))
+    def send_higher():
+        @pl.when(z < n_z - 1)
+        def _():
+            pl.semaphore_wait(later, n_z - 1 - z)
+
+        along_z(early, 8, True)
+        along_z(column, 5, True)
+
+    in_second_half = z >= n_z // 2 - 1
+    waits_less = b == 0
+    parts_first = in_second_half | (y == n_y - 1)
+    parts_step = jnp.where(parts_first, leaves // BLOCK, 1)
+    group_step = jnp.where(parts_first | ((b == 0) & (s != 1)), 2, 3)
+    pl.when(jnp.logical_not(waits_less))(send_higher)
+
     @pl.when(starts_late)
     def _():
         prepare_groups()
-        pl.when(lower_late)(lambda: start_all(down[2:]))
         pl.when(upper_late)(lambda: start_all(up))
 
     def prepare_nodes():
@@ -304,19 +313,19 @@
         for d in range(n_z):
             coeffs += [column[d, :, :NV], column[d, :, NV:]]
         high, low = split(jnp.concatenate(coeffs, 0))
-        fields = dot_bf16(mix[...], jnp.concatenate([high, low, high], 0))
-        for d in range(n_y):
-            at = d * RANK
-            part[d] = jnp.concatenate([fields[at : at + RANK], fields[n_y * RANK + at : n_y * RANK + at + RANK]], 1)
-        for d in ys:
-            remote(part.at[d], parts.at[d], 6, y_peer(d)).start()
+        coeffs = jnp.concatenate([high, low, high], 0)
+        for level, own, k in ((1, group_part, 6), (0, node_part, 11)):
+            fields = dot_bf16(mix[level * n_y * RANK : (level + 1) * n_y * RANK], coeffs)
+            for d in [*ys, 0]:
+                at = d * RANK
+                own[d] = jnp.concatenate([fields[at : at + RANK // 2], fields[at + RANK // 2 : at + RANK]], 1)
+                if d:
+                    remote(own.at[d], (group_parts if level else node_parts).at[d], k, y_peer(d)).start()
 
     def both_parts():
         prepare_nodes()
         send_parts()
 
-    in_second_half = z >= n_z // 2 - 1
-    parts_first = in_second_half | (y == n_y - 1)
     pl.when(parts_first)(both_parts)
     l_near.wait()
 
@@ -375,19 +384,17 @@
                     acc = None
 
     def send_group():
-        remote(parts.at[ny1], parts.at[ny1], 6, y_peer(1)).wait_recv()
-        field = part[0]
+        remote(group_parts.at[ny1], group_parts.at[ny1], 6, y_peer(1)).wait_recv()
+        field = group_part[0]
         for d in ys:
-            field = field + parts[d]
-        own_field[...] = field
-        fc[0] = jnp.concatenate([field[: RANK // 2, NV:], field[RANK // 2 :, NV:]], 1)
+            field = field + group_parts[d]
+        fc[0] = field
         for d in ss:
             remote(fc.at[0], fc.at[d], 7, sub_peer(d)).start()
 
-    parts_step = jnp.where(parts_first, leaves // BLOCK, 1)
-    group_step = jnp.where(in_second_half, 2, 3)
 
     def near_block(t, c):
+        pl.when((t == 1) & waits_less)(send_higher)
         pl.when(t == parts_step)(both_parts)
         pl.when(t == group_step)(send_group)
         near_leaves(t * BLOCK)
@@ -395,27 +402,35 @@
 
     lax.fori_loop(0, leaves // BLOCK, near_block, 0)
 
+    def finish(copies):
+        for copy in copies:
+            copy.wait_send()
+
+    pl.when(has_lower)(lambda: finish(down))
+    pl.when(has_upper)(lambda: finish(up))
+    for ref, k in (
+        (info.at[ny1], 4), (column.at[nz1], 5), (group_parts.at[ny1], 6), (fc.at[ns1], 7), (early.at[nz1], 8),
+        (node_parts.at[ny1], 11),
+    ):
+        remote(ref, ref, k, sub_peer(1)).wait_send()
+
+    remote(node_parts.at[ny1], node_parts.at[ny1], 11, y_peer(1)).wait_recv()
+    field = node_part[0]
+    for d in ys:
+        field = field + node_parts[d]
+    own_field = jnp.concatenate([field[:, :NV], field[:, NV:]], 0)
     remote(fc.at[ns1], fc.at[ns1], 7, sub_peer(1)).wait_recv()
     group = fc[0]
     for d in ss:
         group = group + fc[d]
     group = jnp.concatenate([group[:, :NV], group[:, NV:]], 0)
-    field = own_field[:, :NV] + dot_high(ntr[0], group)
+    field = own_field + dot_high(ntr[0], group)
     fh, fl = split(field.T)
     lhs = jnp.concatenate([fh, fh, fl], 1)
 
     for i in range(leaves // 2):
         cols = pl.ds(i * 2 * LEAF, 2 * LEAF)
         out[:, cols] += dot_bf16(lhs, w3[:, cols])
-
-    def finish(copies):
-        for copy in copies:
-            copy.wait_send()
-
-    pl.when(has_lower)(lambda: finish(down))
-    pl.when(has_upper)(lambda: finish(up))
-    for ref, k in ((info.at[ny1], 4), (column.at[nz1], 5), (parts.at[ny1], 6), (fc.at[ns1], 7), (early.at[nz1], 8)):
-        remote(ref, ref, k, sub_peer(1)).wait_send()
 
 
 def body(sizes, vectors, coords, basis, leaf_transfer, node_transfer, skel_one, skel_two, near_list, list_one, list_two):
@@ -450,13 +465,14 @@
             pltpu.VMEM((n_y * RANK, 8), F32),
             pltpu.VMEM((n_y * RANK, n_z * RANK), F32),
             pltpu.VMEM((2 * n_y * RANK, 3 * n_z * RANK), BF16),
-            pltpu.VMEM((n_y, RANK, 128), F32),
-            pltpu.VMEM((n_y, RANK, 128), F32),
-            pltpu.VMEM((RANK, 128), F32),
+            pltpu.VMEM((n_y, RANK // 2, 128), F32),
+            pltpu.VMEM((n_y, RANK // 2, 128), F32),
+            pltpu.VMEM((n_y, RANK // 2, 128), F32),
+            pltpu.VMEM((n_y, RANK // 2, 128), F32),
             pltpu.VMEM((n_sub, RANK // 2, 128), F32),
             pltpu.SemaphoreType.DMA((10,)),
-            pltpu.SemaphoreType.DMA((11,)),
-            pltpu.SemaphoreType.DMA((11,)),
+            pltpu.SemaphoreType.DMA((12,)),
+            pltpu.SemaphoreType.DMA((12,)),
             pltpu.SemaphoreType.REGULAR,
         ],
         compiler_params=pltpu.CompilerParams(

time: 32.2 us -> 32.2 us (level)
  the two profiles are of different devices: /device:TPU:1 before, /device:TPU:320 now
where the time goes in v6:
time: 32.2 us; the launch traced here: 32.1 us
  Pallas kernels  31.1 us (97%)
  local copies, waits for them, and re-layouts  0.97 us (3%)
    pallas_call x1, Pallas kernels, body(): pl.pallas_call(functools.partial(kernel, sizes), out_shape=pltpu.VMEM(vec...  31.1 us
    unnamed x1, local copies, waits for them, and re-layouts  0.97 us

profile of v6, /device:TPU:320, one launch (start us, length us, event | category | flops | bytes accessed | tf_op | source)
XLA Modules:
  0.0 32.1 jit_solution(6884263601059247851)
XLA Ops:
  0.0 31.1 %h2_product.1 = f32[64,4096]{1,0:T(8,128)S(1)} custom-call(f32[64,4096]{1,0:T(8,128)} %refs_0_.1, f32[2,4096]{1,0:T(2,128)} %refs_1_.1, f32[32,4096]{1,0:T(8,128)} %refs_2_.1, f32[32,32,32]{2,1,0:T(8,128)} %refs_3_.1, f32[1,32,32]{2,1,0:T(8,128)} %refs_4_.1, f32[1,2,32]{2,1,0:T(2,128)} %refs_5_.1, f32[2,32,64]{2,1,0:T(8,128)} %bitcast.2, s32[9,32]{1,0:T(8,128)} %bitcast.3, ...), custom_call_target="tpu_custom_call" | custom-call | tf_op jit(solution)/shard_map/h2_product/pallas_call | solution.py:448
  31.1 1.0 %copy.12 = f32[64,4096]{1,0:T(8,128)} copy(f32[64,4096]{1,0:T(8,128)S(1)} %h2_product.1) | data formatting | bytes 2097152

commit v7 on v6

--- a/solution.py
+++ b/solution.py
@@ -307,24 +307,30 @@
         node_rows = [early[d, 8:9] for d in range(n_z)]
         keep_mix(0, counted_tile(places[:, 0:2], targets(), node_rows, source_names(n_sub, s), 2 * RANK))
 
-    def send_parts():
-        remote(column.at[nz1], column.at[nz1], 5, z_peer(1)).wait_recv()
+    def send_level(level, own, theirs, k):
         coeffs = []
         for d in range(n_z):
             coeffs += [column[d, :, :NV], column[d, :, NV:]]
         high, low = split(jnp.concatenate(coeffs, 0))
         coeffs = jnp.concatenate([high, low, high], 0)
-        for level, own, k in ((1, group_part, 6), (0, node_part, 11)):
-            fields = dot_bf16(mix[level * n_y * RANK : (level + 1) * n_y * RANK], coeffs)
-            for d in [*ys, 0]:
-                at = d * RANK
-                own[d] = jnp.concatenate([fields[at : at + RANK // 2], fields[at + RANK // 2 : at + RANK]], 1)
-                if d:
-                    remote(own.at[d], (group_parts if level else node_parts).at[d], k, y_peer(d)).start()
+        fields = dot_bf16(mix[level * n_y * RANK : (level + 1) * n_y * RANK], coeffs)
+        for d in [*ys, 0]:
+            at = d * RANK
+            own[d] = jnp.concatenate([fields[at : at + RANK // 2], fields[at + RANK // 2 : at + RANK]], 1)
+            if d:
+                remote(own.at[d], theirs.at[d], k, y_peer(d)).start()
+
+    def send_parts():
+        remote(column.at[nz1], column.at[nz1], 5, z_peer(1)).wait_recv()
+        send_level(1, group_part, group_parts, 6)
+
+    def send_nodes():
+        send_level(0, node_part, node_parts, 11)
 
     def both_parts():
         prepare_nodes()
         send_parts()
+        pl.when(jnp.logical_not(starts_late))(send_nodes)
 
     pl.when(parts_first)(both_parts)
     l_near.wait()
@@ -396,6 +402,7 @@
     def near_block(t, c):
         pl.when((t == 1) & waits_less)(send_higher)
         pl.when(t == parts_step)(both_parts)
+        pl.when((t == 1) & starts_late)(send_nodes)
         pl.when(t == group_step)(send_group)
         near_leaves(t * BLOCK)
         return c

time: 32.2 us -> 31.8 us (0.988)
  the two profiles are of different devices: /device:TPU:320 before, /device:TPU:321 now
where the time goes in v7:
time: 31.8 us; the launch traced here: 31.7 us
  Pallas kernels  30.7 us (97%)
  local copies, waits for them, and re-layouts  0.97 us (3%)
    pallas_call x1, Pallas kernels, body(): pl.pallas_call(functools.partial(kernel, sizes), out_shape=pltpu.VMEM(vec...  30.7 us
    unnamed x1, local copies, waits for them, and re-layouts  0.97 us

profile of v7, /device:TPU:321, one launch (start us, length us, event | category | flops | bytes accessed | tf_op | source)
XLA Modules:
  0.0 31.7 jit_solution(16563597070758869821)
XLA Ops:
  0.0 30.7 %h2_product.1 = f32[64,4096]{1,0:T(8,128)S(1)} custom-call(f32[64,4096]{1,0:T(8,128)} %refs_0_.1, f32[2,4096]{1,0:T(2,128)} %refs_1_.1, f32[32,4096]{1,0:T(8,128)} %refs_2_.1, f32[32,32,32]{2,1,0:T(8,128)} %refs_3_.1, f32[1,32,32]{2,1,0:T(8,128)} %refs_4_.1, f32[1,2,32]{2,1,0:T(2,128)} %refs_5_.1, f32[2,32,64]{2,1,0:T(8,128)} %bitcast.2, s32[9,32]{1,0:T(8,128)} %bitcast.3, ...), custom_call_target="tpu_custom_call" | custom-call | tf_op jit(solution)/shard_map/h2_product/pallas_call | solution.py:455
  30.7 1.0 %copy.12 = f32[64,4096]{1,0:T(8,128)} copy(f32[64,4096]{1,0:T(8,128)S(1)} %h2_product.1) | data formatting | bytes 2097152

commit v8 on v7

--- a/solution.py
+++ b/solution.py
@@ -324,13 +324,15 @@
         remote(column.at[nz1], column.at[nz1], 5, z_peer(1)).wait_recv()
         send_level(1, group_part, group_parts, 6)
 
+    nodes_later = starts_late & (y > 0)
+
     def send_nodes():
         send_level(0, node_part, node_parts, 11)
 
     def both_parts():
         prepare_nodes()
         send_parts()
-        pl.when(jnp.logical_not(starts_late))(send_nodes)
+        pl.when(jnp.logical_not(nodes_later))(send_nodes)
 
     pl.when(parts_first)(both_parts)
     l_near.wait()
@@ -402,7 +404,7 @@
     def near_block(t, c):
         pl.when((t == 1) & waits_less)(send_higher)
         pl.when(t == parts_step)(both_parts)
-        pl.when((t == 1) & starts_late)(send_nodes)
+        pl.when((t == 1) & nodes_later)(send_nodes)
         pl.when(t == group_step)(send_group)
         near_leaves(t * BLOCK)
         return c

time: 31.8 us -> 31.9 us (level)
  no operation moved by 1% of the time
where the time goes in v8:
time: 31.9 us; the launch traced here: 31.7 us
  Pallas kernels  30.8 us (97%)
  local copies, waits for them, and re-layouts  0.97 us (3%)
    pallas_call x1, Pallas kernels, body(): pl.pallas_call(functools.partial(kernel, sizes), out_shape=pltpu.VMEM(vec...  30.8 us
    unnamed x1, local copies, waits for them, and re-layouts  0.97 us

profile of v8, /device:TPU:321, one launch (start us, length us, event | category | flops | bytes accessed | tf_op | source)
XLA Modules:
  0.0 31.7 jit_solution(2622738347589951962)
XLA Ops:
  0.0 30.8 %h2_product.1 = f32[64,4096]{1,0:T(8,128)S(1)} custom-call(f32[64,4096]{1,0:T(8,128)} %refs_0_.1, f32[2,4096]{1,0:T(2,128)} %refs_1_.1, f32[32,4096]{1,0:T(8,128)} %refs_2_.1, f32[32,32,32]{2,1,0:T(8,128)} %refs_3_.1, f32[1,32,32]{2,1,0:T(8,128)} %refs_4_.1, f32[1,2,32]{2,1,0:T(2,128)} %refs_5_.1, f32[2,32,64]{2,1,0:T(8,128)} %bitcast.2, s32[9,32]{1,0:T(8,128)} %bitcast.3, ...), custom_call_target="tpu_custom_call" | custom-call | tf_op jit(solution)/shard_map/h2_product/pallas_call | solution.py:457
  30.8 1.0 %copy.12 = f32[64,4096]{1,0:T(8,128)} copy(f32[64,4096]{1,0:T(8,128)S(1)} %h2_product.1) | data formatting | bytes 2097152
